TPU v7x, 256 devices: a whole 4x4x8 slice. The times are simulated.
256 devices in a mesh: cent: 4 (over y_lo, core), pts: 64 (over z, x, y_hi).
Axes of the slice: x: 4, y: 4 (y_hi: 2, y_lo: 2; y = y_hi * 2 + y_lo), z: 8, core: 2. Of those that a mesh axis runs over, the one named last changes fastest.
Arguments:
- points: bfloat16 [96, 32768], P(None, ('cent', 'pts')), may hold values from -60 to 60
- centroids: bfloat16 [96, 65536], P(None, 'cent'), may hold values from -6 to 6
Outputs:
- new_centroids: float32 [96, 65536], P(None, 'cent')
- normalizers: float32 [32768], P(('cent', 'pts'))
All inputs are finite; a program needn't handle non-finite values.
Results may differ from a plain program's by a relative error of at most 0.0065.
The roundings to bfloat16 on the way count: a program that leaves them out, or rounds other values in their place, can miss the bound.
Values may be sent and summed in bfloat16 or wider, within the bound.
A program may use at most 128 MiB of HBM per device.

v0:
```python
import jax
import jax.numpy as jnp
from jax import lax
from jax.sharding import PartitionSpec as P

TEMPER_SCALE = 10.0
PRIOR_MASS = 0.1
EPSILON = 1e-06


def from_behind(value, axis, steps):
    count = lax.axis_size(axis)
    pairs = [(source, (source + steps) % count) for source in range(count)]
    return lax.ppermute(value, axis, pairs)


def unit_columns(centroids):
    as_float = centroids.astype(jnp.float32)
    return (
        as_float * lax.rsqrt(jnp.sum(as_float * as_float, axis=0, keepdims=True) + EPSILON)
    ).astype(jnp.bfloat16)


def column_span():
    return 4096


def combine_stats(earlier, later):
    highest = jnp.maximum(earlier[0], later[0])
    return (
        highest,
        earlier[1] * jnp.exp(earlier[0] - highest) + later[1] * jnp.exp(later[0] - highest),
    )


def block_scores(points_block, unit_cols, offset, col_span):
    return TEMPER_SCALE * jnp.einsum(
        "dn,dk->nk",
        points_block,
        unit_cols[:, offset : offset + col_span],
        preferred_element_type=jnp.float32,
    )


def block_stats(points_block, unit_cols):
    total_cols = unit_cols.shape[1]
    col_span = column_span()
    running = None
    for offset in range(0, total_cols, col_span):
        scores = block_scores(points_block, unit_cols, offset, col_span)
        top_score = jnp.max(scores, axis=1)
        exp_totals = jnp.sum(jnp.exp(scores - top_score[:, None]), axis=1)
        running = (
            (top_score, exp_totals)
            if running is None
            else combine_stats(running, (top_score, exp_totals))
        )
    return running


def block_sums(points_block, normal_log, unit_cols):
    total_cols = unit_cols.shape[1]
    col_span = column_span()
    pieces = []
    masses = []
    for offset in range(0, total_cols, col_span):
        scores = block_scores(points_block, unit_cols, offset, col_span)
        weights = jnp.exp(scores - normal_log[:, None]).astype(jnp.bfloat16)
        pieces.append(
            jnp.einsum("dn,nk->dk", points_block, weights, preferred_element_type=jnp.float32)
        )
        masses.append(jnp.sum(weights.astype(jnp.float32), axis=0))
    return (jnp.concatenate(pieces, axis=1), jnp.concatenate(masses, axis=0))


def finish(weighted_sums, masses, unit_part):
    return (weighted_sums + PRIOR_MASS * unit_part.astype(jnp.float32)) / (masses + PRIOR_MASS)[
        None, :
    ]


def per_device(points, centroids):
    unit_cols = unit_columns(centroids)
    cycle_size = lax.axis_size("cent")
    top_score, exp_totals = block_stats(points, unit_cols)
    moving = (points.astype(jnp.float32), top_score, exp_totals)
    for rounds in range(cycle_size):
        moving = from_behind((moving[0], moving[1], moving[2]), "cent", 1)
        if rounds < cycle_size - 1:
            extra = block_stats(moving[0].astype(jnp.bfloat16), unit_cols)
            merged = combine_stats((moving[1], moving[2]), extra)
            moving = (moving[0], merged[0], merged[1])
    own_log = moving[1] + jnp.log(moving[2])
    weighted_sums, masses = block_sums(points, own_log, unit_cols)
    passing = (points.astype(jnp.float32), own_log)
    for rounds in range(cycle_size - 1):
        passing = from_behind((passing[0], passing[1]), "cent", 1)
        more_sums, more_mass = block_sums(passing[0].astype(jnp.bfloat16), passing[1], unit_cols)
        weighted_sums = weighted_sums + more_sums
        masses = masses + more_mass
    weighted_sums, masses = lax.psum((weighted_sums, masses), "pts")
    updated = finish(weighted_sums, masses, unit_cols)
    return (updated, own_log)


def solution(mesh):
    return jax.shard_map(
        per_device,
        mesh=mesh,
        in_specs=(P(None, ("cent", "pts")), P(None, "cent")),
        out_specs=(P(None, "cent"), P(("cent", "pts"))),
        check_vma=False,
    )
```

profile of v0, /device:TPU:2, one launch (start us, length us, event | category | flops | bytes accessed | tf_op | source)
XLA Modules:
  0.0 824.3 jit_solution(1757411560289725648)
XLA Ops:
  7.3 2.8 fusion
  10.1 0.5 fusion.1
  10.9 0.7 fusion.40
  11.6 0.7 fusion.41
  12.4 0.7 fusion.38
  13.1 0.7 fusion.39
  13.9 0.6 exponential_reduce_fusion.14
  14.4 0.6 exponential_reduce_fusion.12
  15.0 1.6 collective-permute-start
  16.8 0.7 fusion.34
  17.6 0.7 fusion.35
  18.3 0.6 exponential_reduce_fusion.8
  18.9 0.7 fusion.36
  19.6 0.7 fusion.37
  20.4 0.6 exponential_reduce_fusion.10
  20.9 1.0 collective-permute-start.3
  22.2 1.5 collective-permute-start.8
  23.7 1.1 collective-permute-done.3
  24.7 0.7 fusion.30
  25.5 0.7 fusion.31
  26.2 0.6 exponential_reduce_fusion.4
  26.8 0.7 fusion.32
  27.6 0.7 fusion.33
  28.3 0.6 exponential_reduce_fusion.6
  29.0 0.6 collective-permute-start.4
  29.7 2.5 collective-permute-done.5
  32.2 0.7 fusion.28
  33.0 0.7 fusion.29
  33.7 0.6 exponential_reduce_fusion.2
  34.3 0.8 copy-done
  35.1 0.7 fusion.26
  35.8 0.7 fusion.27
  36.6 0.6 exponential_reduce_fusion
  37.1 0.7 copy-done.4
  38.2 0.6 collective-permute-start.6
  38.7 2.4 collective-permute-done.10
  41.3 2.8 convert_reduce_fusion.15
  44.1 0.5 convolution_bitcast_fusion.15
  44.6 1.6 convolution_bitcast_fusion.14
  46.2 1.6 convolution_bitcast_fusion.13
  47.9 1.7 convolution_bitcast_fusion.12
  49.6 0.6 collective-permute-start.12
  50.1 2.2 convert_reduce_fusion.11
  52.4 1.7 convolution_bitcast_fusion.10
  54.1 1.7 convolution_bitcast_fusion.11
  55.7 1.6 convolution_bitcast_fusion.8
  57.4 1.6 convolution_bitcast_fusion.9
  59.2 2.2 convert_reduce_fusion.7
  61.5 1.6 convolution_bitcast_fusion.4
  63.1 1.7 convolution_bitcast_fusion.5
  64.8 1.6 convolution_bitcast_fusion.6
  66.4 1.6 convolution_bitcast_fusion.7
  68.1 0.9 copy-done.1
  69.0 2.2 convert_reduce_fusion.3
  71.2 0.6 fusion.21
  71.9 1.7 convolution_bitcast_fusion
  73.6 1.6 convolution_bitcast_fusion.1
  75.2 1.6 convolution_bitcast_fusion.2
  76.8 0.5 convolution_bitcast_fusion.3
  77.3 0.9 copy-done.8
  78.7 9.9 %fusion.3 = f32[96,16384]{1,0:T(8,128)} fusion(f32[96,4096]{1,0:T(8,128)} %convolution_bitcast_fusion.12, f32[96,4096]{1,0:T(8,128)S(1)} %copy-done.9, f32[96,4096]{1,0:T(8,128)S(1)} %copy-done.8, f32[96,4096]{1,0:T(8,128)S(1)} %convolution_bitcast_fusion.15, f32[96,4096]{1,0:T(8,128)} %convolution_bitcast_fusion.8, f32[96,4096]{1,0:T(8,128)} %convolution_bitcast_fusion.9, ...), kind=kLoop, calls=%fused_computation.6 | loop fusion | flops 23592960 | bytes 31457280 | tf_op jit(solution)/shard_map/add | solution.py:99
  88.6 721.0 %all-reduce.3.cloned.1.call-done = (f32[96,16384]{1,0:T(8,128)}, f32[16384]{0:T(1024)}) async-done(((f32[96,16384]{1,0:T(8,128)}, f32[16384]{0:T(1024)}), (f32[96,16384]{1,0:T(8,128)}, f32[16384]{0:T(1024)})) %all-reduce.3.cloned.1.call-update) | async-done | bytes 6357008 | tf_op jit(solution)/shard_map/psum | solution.py:101
  809.7 0.8 broadcast_add_fusion
  810.6 6.7 add_divide_fusion
  (63 shorter events, 2.1 us)
Async XLA Ops:
  7.2 2.9 copy-start.6
  7.2 802.5 %all-reduce.3.cloned.1.call-start = ((), (), s32[]{:S(2)}) async-start(), calls=%async_computation | async-start | bytes 12713984 | tf_op jit(solution)/shard_map/psum | solution.py:101
  7.2 9.6 %collective-permute-start.1 = (bf16[96,128]{1,0:T(8,128)(2,1)}, bf16[96,128]{1,0:T(8,128)(2,1)S(1)}, u32[]{:S(2)}, u32[]{:S(2)}) collective-permute-start(bf16[96,128]{1,0:T(8,128)(2,1)} %param.2), channel_id=1, source_target_pairs={{0,64},{64,128},{128,192},{192,0},{1,65},{65,129},{129,193},{193,1... | collective-permute-start | bytes 73736 | tf_op jit(solution)/shard_map/ppermute | solution.py:14
  10.1 0.6 copy-start.11
  10.1 0.8 copy-start.10
  15.0 6.9 collective-permute-start
  16.6 5.3 collective-permute-start.7
  20.9 3.8 collective-permute-start.3
  22.0 7.0 collective-permute-start.2
  22.2 6.8 collective-permute-start.8
  28.9 3.3 collective-permute-start.5
  29.0 8.9 %collective-permute-start.4 = (f32[128]{0:T(128)S(1)}, f32[128]{0:T(128)S(1)}, u32[]{:S(2)}, u32[]{:S(2)}) collective-permute-start(f32[128]{0:T(128)S(1)} %get-tuple-element.23), channel_id=1, source_target_pairs={{0,64},{64,128},{128,192},{192,0},{1,65},{65,129},{129,193},{193,1... | collective-permute-start | bytes 1544 | tf_op jit(solution)/shard_map/ppermute | solution.py:14
  29.6 8.2 %collective-permute-start.9 = (f32[128]{0:T(128)S(1)}, f32[128]{0:T(128)S(1)}, u32[]{:S(2)}, u32[]{:S(2)}) collective-permute-start(f32[128]{0:T(128)S(1)} %get-tuple-element.22), channel_id=1, source_target_pairs={{0,64},{64,128},{128,192},{192,0},{1,65},{65,129},{129,193},{193,1... | collective-permute-start | bytes 1544 | tf_op jit(solution)/shard_map/ppermute | solution.py:14
  33.7 1.3 copy-start
  35.8 1.3 copy-start.2
  36.5 1.3 copy-start.4
  37.9 3.2 collective-permute-start.10
  38.2 3.0 collective-permute-start.6
  41.2 6.7 copy-start.17
  41.2 8.3 %collective-permute-start.11 = (f32[128]{0:T(128)S(1)}, f32[128]{0:T(128)S(1)}, u32[]{:S(2)}, u32[]{:S(2)}) collective-permute-start(f32[128]{0:T(128)S(1)} %log_add_fusion), channel_id=1, source_target_pairs={{0,64},{64,128},{128,192},{192,0},{1,65},{65,129},{129,193},{193,1... | collective-permute-start | bytes 1544 | tf_op jit(solution)/shard_map/ppermute | solution.py:14
  49.6 9.5 %collective-permute-start.12 = (f32[128]{0:T(128)S(1)}, f32[128]{0:T(128)S(1)}, u32[]{:S(2)}, u32[]{:S(2)}) collective-permute-start(f32[128]{0:T(128)S(1)} %collective-permute-done.11), channel_id=1, source_target_pairs={{0,64},{64,128},{128,192},{192,0},{1,65},{65,129},{129,193},{193,1... | collective-permute-start | bytes 1544 | tf_op jit(solution)/shard_map/ppermute | solution.py:14
  59.0 9.0 %collective-permute-start.13 = (f32[128]{0:T(128)S(1)}, f32[128]{0:T(128)S(1)}, u32[]{:S(2)}, u32[]{:S(2)}) collective-permute-start(f32[128]{0:T(128)S(1)} %collective-permute-done.12), channel_id=1, source_target_pairs={{0,64},{64,128},{128,192},{192,0},{1,65},{65,129},{129,193},{193,1... | collective-permute-start | bytes 1544 | tf_op jit(solution)/shard_map/ppermute | solution.py:14
  64.8 3.3 copy-start.3
  64.8 3.3 copy-start.5
  66.4 2.5 copy-start.1
  68.1 3.2 copy-start.13
  68.1 3.2 copy-start.14
  68.1 3.2 copy-start.15
  68.1 3.2 copy-start.16
  76.8 1.4 copy-start.8
  76.8 1.9 copy-start.9
  88.6 721.9 %copy-start.7 = (bf16[96,16384]{1,0:T(8,128)(2,1)S(1)}, bf16[96,16384]{1,0:T(8,128)(2,1)}, u32[]{:S(2)}) copy-start(bf16[96,16384]{1,0:T(8,128)(2,1)} %param.3) | copy-start | bytes 9437188
  88.6 721.9 %copy-start.12 = (f32[16384]{0:T(1024)S(1)}, f32[16384]{0:T(1024)}, u32[]{:S(2)}) copy-start(f32[16384]{0:T(1024)} %copy-done.11) | copy-start | bytes 196612
Sparse Core Ops, SparseCore 0:
  88.8 720.8 all-reduce.2
where the time goes:
time: 833 us; the launch traced here: 824 us
  waiting for transfers between devices  727 us (87%)
  matrix products  36 us (4%)
  other arithmetic  35.5 us (4%)
  between operations  14.6 us (2%)
    psum x1, waiting for transfers between devices, per_device(): weighted_sums, masses = lax.psum((weighted_sums, masses), 'pts')  721 us
    dot_general x16, matrix products, block_sums(): jnp.einsum('dn,nk->dk', points_block, weights, preferred_element_type=jnp...  24.1 us
  transfers between devices with their start and end apart: 15, of which 5 were waited for; matrix products, arithmetic and copies ran while one was open for 6% of the time, Pallas kernels for 0%

commit v1 on v0

v1 whole, which is shorter than its diff:
```python
import functools

import jax
import jax.numpy as jnp
from jax import lax
from jax.experimental import pallas as pl
from jax.experimental.pallas import tpu as pltpu
from jax.sharding import Mesh, PartitionSpec as P

TEMPER_SCALE = 10.0
PRIOR_MASS = 0.1
EPSILON = 1e-06
LOG2E = 1.4426950408889634
LN2 = 0.6931471805599453
AXES = ("yl", "core", "z", "x", "yh")
PLANE = ("yl", "core", "z", "yh")
GROUP = ("z", "x", "yh")
BIG = 2048


def unit_columns(centroids):
    as_float = centroids.astype(jnp.float32)
    return (
        as_float * lax.rsqrt(jnp.sum(as_float * as_float, axis=0, keepdims=True) + EPSILON)
    ).astype(jnp.bfloat16)


def stats_kernel(pts_ref, ut_ref, out_ref):
    cols, rows = pts_ref.shape[1], ut_ref.shape[0]
    step = 256

    def block(j, _):
        at = pl.ds(pl.multiple_of(j * BIG, BIG), BIG)
        pts = pts_ref[:, at]
        top = jnp.full((8, BIG), -1e30, jnp.float32)
        total = jnp.zeros((8, BIG), jnp.float32)
        for k in range(0, rows, step):
            s = jnp.dot(ut_ref[k : k + step, :], pts, preferred_element_type=jnp.float32)
            s = s.reshape(step // 8, 8, BIG)
            new = jnp.maximum(top, jnp.max(s, axis=0))
            e = jnp.exp2((s - new[None]) * (TEMPER_SCALE * LOG2E))
            total = total * jnp.exp2((top - new) * (TEMPER_SCALE * LOG2E)) + jnp.sum(e, axis=0)
            top = new
        best = jnp.max(top, axis=0, keepdims=True)
        out_ref[0:1, at] = best
        out_ref[1:2, at] = jnp.sum(
            total * jnp.exp2((top - best) * (TEMPER_SCALE * LOG2E)), axis=0, keepdims=True
        )
        return 0

    lax.fori_loop(0, cols // BIG, block, 0)


def sums_kernel(pts_ref, lse_ref, ut_ref, ptst_ref, out_ref, ext_ref):
    cols, rows = pts_ref.shape[1], ut_ref.shape[0]
    step = 256
    ext_ref[0:96, :] = pts_ref[...]
    a = lse_ref[...] * (-1.0 / TEMPER_SCALE)
    hi = a.astype(jnp.bfloat16).astype(jnp.float32)
    mid = (a - hi).astype(jnp.bfloat16).astype(jnp.float32)
    low = a - hi - mid
    row = lax.broadcasted_iota(jnp.int32, (32, cols), 0)
    extra = jnp.where(row == 0, hi, jnp.where(row == 1, mid, jnp.where(row == 2, low, 0.0)))
    ext_ref[96:128, :] = extra.astype(jnp.bfloat16)
    out_ref[...] = jnp.zeros_like(out_ref)

    def block(j, _):
        at = pl.ds(pl.multiple_of(j * BIG, BIG), BIG)
        pts = ext_ref[:, at]
        ptst = ptst_ref[at, :]
        for k in range(0, rows, step):
            s = jnp.dot(ut_ref[k : k + step, :], pts, preferred_element_type=jnp.float32)
            e = jnp.exp2(s * (TEMPER_SCALE * LOG2E)).astype(jnp.bfloat16)
            out_ref[k : k + step, :] += jnp.dot(e, ptst, preferred_element_type=jnp.float32)
        return 0

    lax.fori_loop(0, cols // BIG, block, 0)


def per_device(points, centroids):
    z, x, yh = lax.axis_index("z"), lax.axis_index("x"), lax.axis_index("yh")
    vmem = pl.BlockSpec(memory_space=pltpu.VMEM)
    params = pltpu.CompilerParams(vmem_limit_bytes=40 * 2**20)
    pts = lax.all_gather(points, PLANE, axis=1, tiled=True)
    mine = jnp.concatenate(
        [
            lax.dynamic_slice_in_dim(centroids, z * 2048 + k * 512 + yh * 256, 256, axis=1)
            for k in range(4)
        ],
        axis=1,
    )
    unit = unit_columns(mine)
    ut = unit.T
    cols, rows = pts.shape[1], ut.shape[0]
    stats = pl.pallas_call(
        stats_kernel,
        out_shape=jax.ShapeDtypeStruct((2, cols), jnp.float32),
        in_specs=[vmem, vmem],
        out_specs=vmem,
        compiler_params=params,
        name="stats",
    )(pts, ut)
    parts = lax.all_to_all(
        stats.reshape(2, 64, 128).transpose(1, 0, 2), PLANE, split_axis=0, concat_axis=0, tiled=True
    )
    best = jnp.max(parts[:, 0], axis=0)
    total = jnp.sum(
        parts[:, 1] * jnp.exp2((parts[:, 0] - best) * (TEMPER_SCALE * LOG2E)), axis=0
    )
    own_log = TEMPER_SCALE * best + jnp.log(total)
    logs = lax.all_gather(own_log, PLANE, axis=0, tiled=True)
    ones = jnp.ones((rows, 3), jnp.bfloat16)
    ut_ext = jnp.concatenate([ut, ones, jnp.zeros((rows, 29), jnp.bfloat16)], axis=1)
    ptst = jnp.concatenate(
        [pts.T, jnp.ones((cols, 1), jnp.bfloat16), jnp.zeros((cols, 31), jnp.bfloat16)], axis=1
    )
    sums = pl.pallas_call(
        sums_kernel,
        out_shape=jax.ShapeDtypeStruct((rows, 128), jnp.float32),
        in_specs=[vmem] * 4,
        out_specs=vmem,
        scratch_shapes=[pltpu.VMEM((128, cols), jnp.bfloat16)],
        compiler_params=params,
        name="sums",
    )(pts, logs.reshape(1, cols), ut_ext, ptst)
    sums = lax.psum_scatter(sums, "x", scatter_dimension=0, tiled=True)
    own_unit = lax.dynamic_slice_in_dim(unit, x * 256, 256, axis=1)
    fresh = (sums[:, :96].T + PRIOR_MASS * own_unit.astype(jnp.float32)) / (
        sums[:, 96] + PRIOR_MASS
    )[None, :]
    whole = lax.all_gather(fresh.astype(jnp.bfloat16), GROUP, axis=1, tiled=True)
    return (whole.astype(jnp.float32), own_log)


def solution(mesh):
    cube = Mesh(mesh.devices.reshape(2, 2, 8, 4, 2), AXES)
    return jax.shard_map(
        per_device,
        mesh=cube,
        in_specs=(P(None, AXES), P(None, ("yl", "core"))),
        out_specs=(P(None, ("yl", "core")), P(AXES)),
        check_vma=False,
    )
```

time: 833 us -> 549 us (0.66); the launches traced: 824 us -> 549 us
  waiting for transfers between devices: 727 us -> 350 us
  blocking collectives: 0 us -> 133 us
  matrix products: 36 us -> 0 us
  other arithmetic: 35.5 us -> 6.91 us
  Pallas kernels: 0 us -> 19.6 us
  local copies, waits for them, and re-layouts: 4.04 us -> 14.2 us
    psum x1 -> x0, waiting for transfers between devices: 721 us -> none  [per_device(): weighted_sums, masses = lax.psum((weighted_sums, masses), 'pts')]
    all_gather x0 -> x2, waiting for transfers between devices: none -> 318 us  [the longest x1 187 us: per_device(): pts = lax.all_gather(points, PLANE, axis=1, tiled=True)]
    all_gather x0 -> x1, blocking collectives: none -> 133 us  [per_device(): logs = lax.all_gather(own_log, PLANE, axis=0, tiled=True)]
    dot_general x32 -> x0, matrix products: 36 us -> none  [the longest x16 24.1 us: block_sums(): jnp.einsum('dn,nk->dk', points_block, weights, preferred_element_type=jnp...]
    reduce_scatter x0 -> x1, waiting for transfers between devices: none -> 25.5 us  [per_device(): sums = lax.psum_scatter(sums, 'x', scatter_dimension=0, tiled=True)]
    pallas_call x0 -> x2, Pallas kernels: none -> 19.6 us  [the longest x1 10.4 us: per_device(): pl.pallas_call(sums_kernel, out_shape=jax.ShapeDtypeStruct((rows, 128), j...]
    reduce_sum x12 -> x1, other arithmetic: 14.1 us -> 0.04 us  [per_device(): jnp.sum(parts[:, 1] * jnp.exp2((parts[:, 0] - best) * (TEMPER_SCALE * LOG...]
    all_to_all x0 -> x1, starting transfers between devices: none -> 10.8 us  [per_device(): lax.all_to_all(stats.reshape(2, 64, 128).transpose(1, 0, 2), PLANE, split...]
  transfers between devices with their start and end apart: 15 -> 4, of which waited for: 5 -> 4; matrix products, arithmetic and copies ran while one was open for 6% -> 1% of each run, Pallas kernels for 0% -> 0%
where the time goes in v1:
time: 549 us
  waiting for transfers between devices  350 us (64%)
  blocking collectives  133 us (24%)
  Pallas kernels  19.6 us (4%)
  local copies, waits for them, and re-layouts  14.2 us (3%)
  between operations  13.9 us (3%)
  starting transfers between devices  10.9 us (2%)
  other arithmetic  6.91 us (1%)
    all_gather x1, waiting for transfers between devices, per_device(): pts = lax.all_gather(points, PLANE, axis=1, tiled=True)  187 us
    all_gather x1, blocking collectives, per_device(): logs = lax.all_gather(own_log, PLANE, axis=0, tiled=True)  133 us
    all_gather x1, waiting for transfers between devices, per_device(): lax.all_gather(fresh.astype(jnp.bfloat16), GROUP, axis=1, tiled=True)  131 us
    reduce_scatter x1, waiting for transfers between devices, per_device(): sums = lax.psum_scatter(sums, 'x', scatter_dimension=0, tiled=True)  25.5 us
  transfers between devices with their start and end apart: 4, of which 4 were waited for; matrix products, arithmetic and copies ran while one was open for 1% of the time, Pallas kernels for 0%

profile of v1, /device:TPU:2, one launch (start us, length us, event | category | flops | bytes accessed | tf_op | source)
XLA Modules:
  0.0 548.8 jit_solution(12148682900025644246)
XLA Ops:
  7.2 0.0 all-gather.4.cloned.1.call-start
  7.2 1.5 copy.20
  8.7 0.0 all-gather.4.cloned.1.call-update
  8.7 0.1 pad.1.clone
  8.8 0.1 pad.4.clone
  8.9 0.1 pad.2.clone
  9.0 0.1 pad.5.clone
  9.0 0.9 constant_dynamic-slice_fusion.3
  9.9 0.1 copy.30
  10.0 0.1 copy.32
  10.2 0.1 copy.31
  10.3 0.1 copy.33
  10.4 0.2 fusion
  10.6 0.2 fusion.1
  10.9 0.1 maximum_maximum_fusion.1.ut_ref
  11.0 187.1 %all-gather.4.cloned.1.call-done = bf16[96,8192]{0,1:T(8,128)(2,1)} async-done(((bf16[96,128]{0,1:T(8,128)(2,1)}), bf16[96,8192]{0,1:T(8,128)(2,1)}) %all-gather.4.cloned.1.call-update) | async-done | bytes 1572880 | tf_op jit(solution)/shard_map/all_gather | solution.py:84
  198.0 2.9 copy.28.pts_ref
  200.9 9.2 %stats.1 = f32[2,8192]{1,0:T(2,128)} custom-call(bf16[96,8192]{1,0:T(8,128)(2,1)S(1)} %copy.28.pts_ref, bf16[1024,96]{1,0:T(8,128)(2,1)S(1)} %bitcast.21), custom_call_target="tpu_custom_call" | custom-call | tf_op jit(solution)/shard_map/stats/pallas_call | solution.py:95
  210.1 10.8 %all-to-all-start = ((f32[64,2,128]{2,1,0:T(2,128)}), f32[64,2,128]{2,1,0:T(2,128)S(1)}, u32[]{:S(2)}, u32[]{:S(2)}) async-start(f32[64,2,128]{2,1,0:T(2,128)} %bitcast.2), calls=%async_computation | async-start | bytes 131072 | tf_op jit(solution)/shard_map/all_to_all | solution.py:103
  220.9 0.0 reduce-scatter.2.cloned.1.call-start
  220.9 3.6 maximum_maximum_fusion.ptst_ref
  224.5 6.3 %all-to-all-done = f32[64,2,128]{2,1,0:T(2,128)S(1)} async-done(((f32[64,2,128]{2,1,0:T(2,128)}), f32[64,2,128]{2,1,0:T(2,128)S(1)}, u32[]{:S(2)}, u32[]{:S(2)}) %all-to-all-start) | async-done | bytes 65568 | tf_op jit(solution)/shard_map/all_to_all | solution.py:103
  230.8 0.1 fusion.6
  231.0 0.0 copy-start.1
  231.0 133.4 %all-gather = f32[64,1,128]{2,1,0:T(1,128)S(1)} all-gather(f32[1,1,128]{2,1,0:T(1,128)S(1)} %bitcast.27), channel_id=1, replica_groups=mesh['yl'=2,'core'=2,'z'=8,'x'=4,'yh'=2] {'yl','core','z','yh'}, dimensions={0}, use_global_device_ids=true | all-gather | bytes 33280 | tf_op jit(solution)/shard_map/all_gather | solution.py:111
  364.3 0.0 copy-start
  364.3 1.6 copy-done
  365.9 10.4 %sums.1 = f32[1024,128]{1,0:T(8,128)} custom-call(bf16[96,8192]{1,0:T(8,128)(2,1)S(1)} %copy.28.pts_ref, f32[1,8192]{1,0:T(1,128)S(1)} %bitcast.22, bf16[1024,128]{1,0:T(8,128)(2,1)S(1)} %maximum_maximum_fusion.1.ut_ref, bf16[8192,128]{1,0:T(8,128)(2,1)S(1)} %copy-done), custom_call_target="tpu_custom_call" | custom-call | tf_op jit(solution)/shard_map/sums/pallas_call | solution.py:117
  376.4 0.0 reduce-scatter.2.cloned.1.call-update
  376.4 0.0 all-gather.6.cloned.1.call-start
  376.4 25.5 %reduce-scatter.2.cloned.1.call-done = f32[256,128]{1,0:T(8,128)} async-done(((f32[1024,128]{1,0:T(8,128)}), f32[256,128]{1,0:T(8,128)}) %reduce-scatter.2.cloned.1.call-update) | async-done | bytes 131088 | tf_op jit(solution)/shard_map/reduce_scatter | solution.py:126
  401.9 1.1 fusion.2
  403.0 1.6 fusion.5
  404.6 0.0 all-gather.6.cloned.1.call-update
  404.7 131.0 %all-gather.6.cloned.1.call-done = bf16[96,16384]{0,1:T(8,128)(2,1)} async-done(((bf16[96,256]{0,1:T(8,128)(2,1)}), bf16[96,16384]{0,1:T(8,128)(2,1)}) %all-gather.6.cloned.1.call-update) | async-done | bytes 3145744 | tf_op jit(solution)/shard_map/all_gather | solution.py:131
  535.6 6.6 %copy.29 = f32[96,16384]{1,0:T(8,128)} copy(bf16[96,16384]{0,1:T(8,128)(2,1)} %all-gather.6.cloned.1.call-done) | data formatting | bytes 9437184
  542.2 0.0 copy-done.1
  (7 shorter events, 0.1 us)
Async XLA Ops:
  7.2 190.9 %all-gather.4.cloned.1.call-start = ((), (), s32[]{:S(2)}) async-start(), calls=%async_computation.2 | async-start | bytes 2129920 | tf_op jit(solution)/shard_map/all_gather | solution.py:84
  210.1 20.8 %all-to-all-start = ((f32[64,2,128]{2,1,0:T(2,128)}), f32[64,2,128]{2,1,0:T(2,128)S(1)}, u32[]{:S(2)}, u32[]{:S(2)}) async-start(f32[64,2,128]{2,1,0:T(2,128)} %bitcast.2), calls=%async_computation | async-start | bytes 131072 | tf_op jit(solution)/shard_map/all_to_all | solution.py:103
  220.9 181.0 %reduce-scatter.2.cloned.1.call-start = ((), (), s32[]{:S(2)}) async-start(), calls=%async_computation.3 | async-start | bytes 655360 | tf_op jit(solution)/shard_map/reduce_scatter | solution.py:126
  231.0 311.3 %copy-start.1 = (f32[128]{0:T(128)}, f32[128]{0:T(128)S(1)}, u32[]{:S(2)}) copy-start(f32[128]{0:T(128)S(1)} %log_add_fusion) | copy-start | bytes 1540
  364.3 1.6 copy-start
  376.4 159.2 %all-gather.6.cloned.1.call-start = ((), (), s32[]{:S(2)}) async-start(), calls=%async_computation.4 | async-start | bytes 4259840 | tf_op jit(solution)/shard_map/all_gather | solution.py:131
Sparse Core Ops, SparseCore 0:
  10.4 187.5 all-gather.3
  376.5 25.3 reduce-scatter.1
  406.0 129.5 all-gather.5

commit v2 on v0

v2 whole, which is shorter than its diff:
```python
import functools

import jax
import jax.numpy as jnp
from jax import lax
from jax.experimental import pallas as pl
from jax.experimental.pallas import tpu as pltpu
from jax.sharding import Mesh, PartitionSpec as P

TEMPER_SCALE = 10.0
PRIOR_MASS = 0.1
EPSILON = 1e-06
LOG2E = 1.4426950408889634
LN2 = 0.6931471805599453
SCALE = TEMPER_SCALE * LOG2E
AXES = ("yl", "core", "z", "x", "yh")
MESH = pl.DeviceIdType.MESH
D = 96
HALF = 2048
BF = jnp.bfloat16
F32 = jnp.float32


def em_kernel(
    points, cents, g, own_log,
    pg, cu, ut, ue, ptst, pe, lp, rxa, cb, rxb, lo, w, rxr,
    cu_sem, ps, pr, ds, dr, bs, br, rs, rr, zs, zr, xs, xr, fs, fr,
):
    yl, core, z, x, yh = [lax.axis_index(a) for a in AXES]
    y = yh * 2 + yl
    chip = x * 4 + y

    def at_plane(i):
        tx, ty = lax.rem(x + i // 4, 4), lax.rem(y + i % 4, 4)
        return (lax.rem(ty, 2), core, z, tx, ty // 2)

    def at_z(i):
        return (yl, core, lax.rem(z + i, 8), x, yh)

    def at_x(i):
        return (yl, core, z, lax.rem(x + i, 4), yh)

    other = (yl, 1 - core, z, x, yh)
    across = (yl, core, z, x, 1 - yh)

    def remote(src, dst, s, r, to):
        return pltpu.make_async_remote_copy(
            src_ref=src, dst_ref=dst, send_sem=s, recv_sem=r, device_id=to, device_id_type=MESH
        )

    loads = []
    for c in range(2):
        for k in range(8):
            col = pl.multiple_of(k * 2048 + (x * 2 + yh) * 256 + c * 128, 128)
            n = c * 8 + k
            cp = pltpu.make_async_copy(
                cents.at[:, pl.ds(col, 128)], cu.at[:, n * 128 : n * 128 + 128], cu_sem.at[n]
            )
            cp.start()
            loads.append(cp)

    barrier = pltpu.get_barrier_semaphore()
    peers = [at_plane(i) for i in range(1, 16)] + [other] + [at_z(i) for i in range(1, 8)]
    for to in peers:
        pl.semaphore_signal(barrier, inc=1, device_id=to, device_id_type=MESH)
    pl.semaphore_wait(barrier, len(peers))

    mine = pl.ds(pl.multiple_of(chip * 128, 128), 128)
    sends = []
    for i in range(1, 16):
        cp = remote(points, pg.at[core, :, mine], ps.at[i], pr.at[i], at_plane(i))
        cp.start()
        sends.append(cp)
    pg[core, :, mine] = points[...]

    for cp in loads:
        cp.wait()
    ue[D:128, :] = jnp.where(
        lax.broadcasted_iota(jnp.int32, (32, 2048), 0) < 3, 1.0, 0.0
    ).astype(BF)
    for k in range(0, 2048, 512):
        f = cu[:, k : k + 512].astype(F32)
        u = (f * lax.rsqrt(jnp.sum(f * f, axis=0, keepdims=True) + EPSILON)).astype(BF)
        ue[0:D, k : k + 512] = u
        full = jnp.concatenate([u.astype(F32), jnp.zeros((32, 512), F32)], axis=0)
        ut[k : k + 512, :] = full.T.astype(BF)

    for cp in sends:
        cp.wait()
    swap = remote(pg.at[core], pg.at[core], ds.at[0], dr.at[0], other)
    swap.start()

    def stats(h):
        pts = pg[h]
        top = jnp.full((8, HALF), -1e30, F32)
        total = jnp.zeros((8, HALF), F32)
        for k in range(0, 2048, 256):
            s = jnp.dot(ut[k : k + 256, 0:D], pts, preferred_element_type=F32)
            s = s.reshape(32, 8, HALF)
            new = jnp.maximum(top, jnp.max(s, axis=0))
            e = jnp.exp2((s - new[None]) * SCALE)
            total = total * jnp.exp2((top - new) * SCALE) + jnp.sum(e, axis=0)
            top = new
        best = jnp.max(top, axis=0, keepdims=True)
        sums = jnp.sum(total * jnp.exp2((top - best) * SCALE), axis=0, keepdims=True)
        lp[h] = best * SCALE + jnp.log2(sums)

    stats(core)
    swap.wait()
    stats(1 - core)

    give = remote(lp.at[1 - core], rxa, ds.at[1], dr.at[1], other)
    give.start()
    ones = jnp.where(lax.broadcasted_iota(jnp.int32, (16, HALF), 0) < 1, 1.0, 0.0).astype(BF)
    for h in range(2):
        pe[h, 0:D, :] = pg[h]
        pe[h, D:112, :] = ones
    give.wait()
    a, b = lp[core], rxa[...]
    top = jnp.maximum(a, b)
    cb[...] = top + jnp.log2(jnp.exp2(a - top) + jnp.exp2(b - top))
    sends = []
    for i in range(1, 16):
        cp = remote(cb, rxb.at[i], bs.at[i], br.at[i], at_plane(i))
        cp.start()
        sends.append(cp)
    rxb[0] = cb[...]
    for h in range(2):
        for k in range(0, HALF, 512):
            f = jnp.concatenate(
                [pg[h, :, k : k + 512].astype(F32), jnp.zeros((32, 512), F32)], axis=0
            )
            ptst[h * HALF + k : h * HALF + k + 512, :] = f.T.astype(BF)
    for cp in sends:
        cp.wait()
    top = rxb[0]
    for i in range(1, 16):
        top = jnp.maximum(top, rxb[i])
    total = jnp.exp2(rxb[0] - top)
    for i in range(1, 16):
        total = total + jnp.exp2(rxb[i] - top)
    lo[core] = top + jnp.log2(total)
    back = remote(lo.at[core], lo.at[core], ds.at[2], dr.at[2], other)
    back.start()
    own_log[...] = lo[core, :, mine] * LN2
    back.wait()

    row = lax.broadcasted_iota(jnp.int32, (32, 512), 0)
    for h in range(2):
        for k in range(0, HALF, 512):
            v = lo[h, :, k : k + 512] * (-1.0 / SCALE)
            hi = v.astype(BF).astype(F32)
            mid = (v - hi).astype(BF).astype(F32)
            low = v - hi - mid
            f = jnp.where(row == 0, hi, jnp.where(row == 1, mid, jnp.where(row == 2, low, 0.0)))
            ptst[h * HALF + k : h * HALF + k + 512, D:128] = f.T.astype(BF)

    def sums(c):
        for q in range(2):
            at = c * 1024 + q * 512
            uk = ue[:, at : at + 512]

            def block(j, acc):
                n = pl.ds(pl.multiple_of(j * 1024, 1024), 1024)
                m = pl.ds(pl.multiple_of(lax.rem(j, 2) * 1024, 1024), 1024)
                s = jnp.dot(ptst[n, :], uk, preferred_element_type=F32)
                e = jnp.exp2(s * SCALE).astype(BF)
                return acc + jnp.dot(pe[j // 2, :, m], e, preferred_element_type=F32)

            acc = lax.fori_loop(0, 4, block, jnp.zeros((112, 512), F32))
            for k in range(4):
                w[c, q * 4 + k] = acc[0:104, k * 128 : k * 128 + 128]

    def reduce_start(c):
        cps = []
        for i in (4, 3, 5, 2, 6, 1, 7):
            zz = lax.rem(z + i, 8)
            cp = remote(w.at[c, zz], rxr.at[c, i], rs.at[c, i], rr.at[c, i], at_z(i))
            cp.start()
            cps.append(cp)
        return cps

    def finish(c):
        acc = w[c, z]
        for i in range(1, 8):
            acc = acc + rxr[c, i]
        u = ue[0:D, pl.ds(pl.multiple_of(c * 1024 + z * 128, 128), 128)].astype(F32)
        g[c, x, yh, z] = ((acc[0:D] + PRIOR_MASS * u) / (acc[D : D + 1] + PRIOR_MASS)).astype(BF)

    def along_z(c):
        cps = []
        for i in (4, 3, 5, 2, 6, 1, 7):
            slot = g.at[c, x, yh, z]
            cp = remote(slot, slot, zs.at[c, i], zr.at[c, i], at_z(i))
            cp.start()
            cps.append(cp)
        return cps

    def region(c, xx, hh, s, r, to):
        cp = remote(g.at[c, xx, hh], g.at[c, xx, hh], s, r, to)
        cp.start()
        return cp

    def spread(c):
        first = region(c, x, yh, xs.at[c, 0], xr.at[c, 0], across)
        return [first] + [
            region(c, x, yh, xs.at[c, i], xr.at[c, i], at_x(i)) for i in (2, 1, 3)
        ]

    sums(0)
    red0 = reduce_start(0)
    sums(1)
    red1 = reduce_start(1)
    for cp in red0:
        cp.wait()
    finish(0)
    z0 = along_z(0)
    for cp in red1:
        cp.wait()
    finish(1)
    z1 = along_z(1)
    for cp in z0:
        cp.wait()
    s0 = spread(0)
    for cp in z1:
        cp.wait()
    s1 = spread(1)
    fwd = []
    s1[0].wait_recv()
    for i in (2, 1, 3):
        fwd.append(region(1, x, 1 - yh, fs.at[1, i], fr.at[1, i], at_x(i)))
    for n, i in ((2, 1), (3, 3), (1, 2)):
        s0[n].wait_recv()
        xx = lax.rem(x + 4 - i, 4)
        fwd.append(region(0, xx, yh, fs.at[0, i], fr.at[0, i], across))
    s0[0].wait_recv()
    for cp in s1[1:]:
        cp.wait_recv()
    for cp in s0 + s1:
        cp.wait_send()
    for cp in fwd:
        cp.wait()


def widen_kernel(g, out):
    for c in range(2):
        for hh in range(2):
            at = (hh * 2 + c) * 128
            out[:, at : at + 128] = g[c, 0, hh, 0].astype(F32)


def per_device(points, centroids):
    vmem = pl.BlockSpec(memory_space=pltpu.VMEM)
    dma = pltpu.SemaphoreType.DMA
    g, own_log = pl.pallas_call(
        em_kernel,
        out_shape=[
            jax.ShapeDtypeStruct((2, 4, 2, 8, D, 128), BF),
            jax.ShapeDtypeStruct((1, 128), F32),
        ],
        in_specs=[vmem, pl.BlockSpec(memory_space=pl.ANY)],
        out_specs=[vmem, vmem],
        scratch_shapes=[
            pltpu.VMEM((2, D, HALF), BF),
            pltpu.VMEM((D, 2048), BF),
            pltpu.VMEM((2048, 128), BF),
            pltpu.VMEM((128, 2048), BF),
            pltpu.VMEM((2 * HALF, 128), BF),
            pltpu.VMEM((2, 112, HALF), BF),
            pltpu.VMEM((2, 1, HALF), F32),
            pltpu.VMEM((1, HALF), F32),
            pltpu.VMEM((1, HALF), F32),
            pltpu.VMEM((16, 1, HALF), F32),
            pltpu.VMEM((2, 1, HALF), F32),
            pltpu.VMEM((2, 8, 104, 128), F32),
            pltpu.VMEM((2, 8, 104, 128), F32),
            dma((16,)), dma((16,)), dma((16,)), dma((3,)), dma((3,)), dma((16,)), dma((16,)),
            dma((2, 8)), dma((2, 8)), dma((2, 8)), dma((2, 8)), dma((2, 4)), dma((2, 4)),
            dma((2, 4)), dma((2, 4)),
        ],
        compiler_params=pltpu.CompilerParams(
            collective_id=0, has_side_effects=True, vmem_limit_bytes=48 * 2**20
        ),
        name="em",
    )(points, centroids)
    whole = pl.pallas_call(
        widen_kernel,
        grid=(8, 4),
        out_shape=jax.ShapeDtypeStruct((D, 16384), F32),
        in_specs=[pl.BlockSpec((2, 1, 2, 1, D, 128), lambda z, x: (0, x, 0, z, 0, 0))],
        out_specs=pl.BlockSpec((D, 512), lambda z, x: (0, z * 4 + x)),
        name="widen",
    )(g)
    return (whole, own_log.reshape(128))


def solution(mesh):
    cube = Mesh(mesh.devices.reshape(2, 2, 8, 4, 2), AXES)
    return jax.shard_map(
        per_device,
        mesh=cube,
        in_specs=(P(None, AXES), P(None, ("yl", "core"))),
        out_specs=(P(None, ("yl", "core")), P(AXES)),
        check_vma=False,
    )
```

time: 833 us -> 115 us (0.14)
  waiting for transfers between devices: 727 us -> 0 us
  Pallas kernels: 0 us -> 110 us
  matrix products: 36 us -> 0 us
  other arithmetic: 35.5 us -> 0 us
  between operations: 14.6 us -> 0.66 us
    psum x1 -> x0, waiting for transfers between devices: 721 us -> none  [per_device(): weighted_sums, masses = lax.psum((weighted_sums, masses), 'pts')]
    pallas_call x0 -> x2, Pallas kernels: none -> 110 us  [the longest x1 92.3 us: per_device(): pl.pallas_call(em_kernel, out_shape=[jax.ShapeDtypeStruct((2, 4, 2, 8, D,...]
    dot_general x32 -> x0, matrix products: 36 us -> none  [the longest x16 24.1 us: block_sums(): jnp.einsum('dn,nk->dk', points_block, weights, preferred_element_type=jnp...]
    reduce_sum x13 -> x0, other arithmetic: 16.9 us -> none  [the longest x4 9.55 us: block_sums(): masses.append(jnp.sum(weights.astype(jnp.float32), axis=0))]
    add x8 -> x0, other arithmetic: 11.4 us -> none  [the longest x1 9.88 us: per_device(): weighted_sums = weighted_sums + more_sums]
  transfers between devices with their start and end apart: 15 -> 0, of which waited for: 5 -> 0; matrix products, arithmetic and copies ran while one was open for 6% -> 0% of each run, Pallas kernels for 0% -> 0%
where the time goes in v2:
time: 115 us; the launch traced here: 114 us
  Pallas kernels  110 us (96%)
  local copies, waits for them, and re-layouts  2.89 us (3%)
    pallas_call x1, Pallas kernels, per_device(): pl.pallas_call(em_kernel, out_shape=[jax.ShapeDtypeStruct((2, 4, 2, 8, D,...  92.3 us
    pallas_call x1, Pallas kernels, per_device(): pl.pallas_call(widen_kernel, grid=(8, 4), out_shape=jax.ShapeDtypeStruct(...  18 us
    unnamed x5, local copies, waits for them, and re-layouts  2.89 us

profile of v2, /device:TPU:2, one launch (start us, length us, event | category | flops | bytes accessed | tf_op | source)
XLA Modules:
  0.0 113.9 jit_solution(17247690262932463813)
XLA Ops:
  0.6 0.0 copy-start.1
  0.6 0.7 copy-done.1
  1.4 92.3 %em.1 = (bf16[2,4,2,8,96,128]{5,4,3,2,1,0:T(8,128)(2,1)S(1)}, f32[1,128]{1,0:T(1,128)S(1)}) custom-call(bf16[96,128]{1,0:T(8,128)(2,1)S(1)} %copy-done.1, bf16[96,16384]{1,0:T(8,128)(2,1)} %cents.1), custom_call_target="tpu_custom_call" | custom-call | tf_op jit(solution)/shard_map/em/pallas_call | solution.py:255
  93.7 0.0 copy-start
  93.7 1.6 %copy-done = bf16[2,4,2,8,96,128]{5,4,3,2,1,0:T(8,128)(2,1)} copy-done((bf16[2,4,2,8,96,128]{5,4,3,2,1,0:T(8,128)(2,1)}, bf16[2,4,2,8,96,128]{5,4,3,2,1,0:T(8,128)(2,1)S(1)}, u32[]{:S(2)}) %copy-start) | copy-done | bytes 3145752
  95.3 18.0 %widen.1 = f32[96,16384]{1,0:T(8,128)} custom-call(bf16[2,4,2,8,96,128]{5,4,3,2,1,0:T(8,128)(2,1)} %copy-done), custom_call_target="tpu_custom_call" | custom-call | tf_op jit(solution)/shard_map/widen/pallas_call | solution.py:286
  113.3 0.5 copy.5
Async XLA Ops:
  0.6 0.7 copy-start.1
  93.7 1.7 %copy-start = (bf16[2,4,2,8,96,128]{5,4,3,2,1,0:T(8,128)(2,1)}, bf16[2,4,2,8,96,128]{5,4,3,2,1,0:T(8,128)(2,1)S(1)}, u32[]{:S(2)}) copy-start(bf16[2,4,2,8,96,128]{5,4,3,2,1,0:T(8,128)(2,1)S(1)} %get-tuple-element.4.g) | copy-start | bytes 9437188

commit v3 on v2

--- a/solution.py
+++ b/solution.py
@@ -23,8 +23,8 @@
 
 def em_kernel(
     points, cents, g, own_log,
-    pg, cu, ut, ue, ptst, pe, lp, rxa, cb, rxb, lo, w, rxr,
-    cu_sem, ps, pr, ds, dr, bs, br, rs, rr, zs, zr, xs, xr, fs, fr,
+    stage, pg, cu, ut, ue, ptst, pe, lp, rxa, cb, rxb, lo, w, wb, rxr,
+    cu_sem, ps, pr, ds, dr, bs, br, rs, rr, zs, zr, gs, gr,
 ):
     yl, core, z, x, yh = [lax.axis_index(a) for a in AXES]
     y = yh * 2 + yl
@@ -59,6 +59,8 @@
             cp.start()
             loads.append(cp)
 
+    own = pltpu.make_async_copy(points, stage, cu_sem.at[16])
+    own.start()
     barrier = pltpu.get_barrier_semaphore()
     peers = [at_plane(i) for i in range(1, 16)] + [other] + [at_z(i) for i in range(1, 8)]
     for to in peers:
@@ -66,12 +68,14 @@
     pl.semaphore_wait(barrier, len(peers))
 
     mine = pl.ds(pl.multiple_of(chip * 128, 128), 128)
-    sends = []
-    for i in range(1, 16):
-        cp = remote(points, pg.at[core, :, mine], ps.at[i], pr.at[i], at_plane(i))
+    order = (1, 2, 3, 4, 5, 6, 7, 12, 13, 14, 15, 8, 9, 10, 11)
+    own.wait()
+    sends = {}
+    for i in order:
+        cp = remote(stage, pg.at[core, :, mine], ps.at[i], pr.at[i], at_plane(i))
         cp.start()
-        sends.append(cp)
-    pg[core, :, mine] = points[...]
+        sends[i] = cp
+    pg[core, :, mine] = stage[...]
 
     for cp in loads:
         cp.wait()
@@ -85,33 +89,46 @@
         full = jnp.concatenate([u.astype(F32), jnp.zeros((32, 512), F32)], axis=0)
         ut[k : k + 512, :] = full.T.astype(BF)
 
-    for cp in sends:
-        cp.wait()
-    swap = remote(pg.at[core], pg.at[core], ds.at[0], dr.at[0], other)
-    swap.start()
-
-    def stats(h):
-        pts = pg[h]
-        top = jnp.full((8, HALF), -1e30, F32)
-        total = jnp.zeros((8, HALF), F32)
-        for k in range(0, 2048, 256):
-            s = jnp.dot(ut[k : k + 256, 0:D], pts, preferred_element_type=F32)
-            s = s.reshape(32, 8, HALF)
+    def column(k):
+        return pl.ds(pl.multiple_of(lax.rem(x + 4 - k, 4) * 512, 512), 512)
+
+    def stats(h, k):
+        pts = pg[h, :, column(k)]
+        top = jnp.full((8, 512), -1e30, F32)
+        total = jnp.zeros((8, 512), F32)
+        for r in range(0, 2048, 256):
+            s = jnp.dot(ut[r : r + 256, 0:D], pts, preferred_element_type=F32)
+            s = s.reshape(32, 8, 512)
             new = jnp.maximum(top, jnp.max(s, axis=0))
             e = jnp.exp2((s - new[None]) * SCALE)
             total = total * jnp.exp2((top - new) * SCALE) + jnp.sum(e, axis=0)
             top = new
         best = jnp.max(top, axis=0, keepdims=True)
         sums = jnp.sum(total * jnp.exp2((top - best) * SCALE), axis=0, keepdims=True)
-        lp[h] = best * SCALE + jnp.log2(sums)
-
-    stats(core)
-    swap.wait()
-    stats(1 - core)
+        lp[h, :, column(k)] = best * SCALE + jnp.log2(sums)
+
+    swaps, before = [], None
+    for n, k in enumerate((0, 1, 3, 2)):
+        for i in range(4 * k, 4 * k + 4):
+            if i:
+                sends[i].wait_recv()
+        part = pg.at[core, :, column(k)]
+        swap = remote(part, part, ds.at[3 + n], dr.at[3 + n], other)
+        swap.start()
+        if before is not None:
+            swaps[-1].wait_recv()
+            stats(1 - core, before)
+        swaps.append(swap)
+        stats(core, k)
+        before = k
+    swaps[-1].wait_recv()
+    stats(1 - core, before)
+    for cp in list(sends.values()) + swaps:
+        cp.wait_send()
 
     give = remote(lp.at[1 - core], rxa, ds.at[1], dr.at[1], other)
     give.start()
-    ones = jnp.where(lax.broadcasted_iota(jnp.int32, (16, HALF), 0) < 1, 1.0, 0.0).astype(BF)
+    ones = jnp.where(lax.broadcasted_iota(jnp.int32, (16, HALF), 0) < 2, 1.0, 0.0).astype(BF)
     for h in range(2):
         pe[h, 0:D, :] = pg[h]
         pe[h, D:112, :] = ones
@@ -168,14 +185,21 @@
                 return acc + jnp.dot(pe[j // 2, :, m], e, preferred_element_type=F32)
 
             acc = lax.fori_loop(0, 4, block, jnp.zeros((112, 512), F32))
+            tail = acc[D:112]
+            hi = tail.astype(BF).astype(F32)
+            first = lax.broadcasted_iota(jnp.int32, (16, 512), 0) == 0
+            parts = jnp.where(first, hi, tail - hi).astype(BF)
             for k in range(4):
-                w[c, q * 4 + k] = acc[0:104, k * 128 : k * 128 + 128]
+                at = slice(k * 128, k * 128 + 128)
+                w[c, q * 4 + k] = acc[0:104, at]
+                wb[c, q * 4 + k, 0:D] = acc[0:D, at].astype(BF)
+                wb[c, q * 4 + k, D:112] = parts[:, at]
 
     def reduce_start(c):
         cps = []
         for i in (4, 3, 5, 2, 6, 1, 7):
             zz = lax.rem(z + i, 8)
-            cp = remote(w.at[c, zz], rxr.at[c, i], rs.at[c, i], rr.at[c, i], at_z(i))
+            cp = remote(wb.at[c, zz], rxr.at[c, i], rs.at[c, i], rr.at[c, i], at_z(i))
             cp.start()
             cps.append(cp)
         return cps
@@ -183,70 +207,110 @@
     def finish(c):
         acc = w[c, z]
         for i in range(1, 8):
-            acc = acc + rxr[c, i]
+            acc = acc + rxr[c, i, 0:104].astype(F32)
+        sums, mass = acc[0:D], acc[D : D + 1] + (acc[D + 1 : D + 2] - w[c, z, D + 1 : D + 2])
         u = ue[0:D, pl.ds(pl.multiple_of(c * 1024 + z * 128, 128), 128)].astype(F32)
-        g[c, x, yh, z] = ((acc[0:D] + PRIOR_MASS * u) / (acc[D : D + 1] + PRIOR_MASS)).astype(BF)
+        g[c, x, yh, z] = ((sums + PRIOR_MASS * u) / (mass + PRIOR_MASS)).astype(BF)
 
     def along_z(c):
-        cps = []
-        for i in (4, 3, 5, 2, 6, 1, 7):
+        cps = {}
+        for i in (1, 7, 2, 6, 3, 5, 4):
             slot = g.at[c, x, yh, z]
             cp = remote(slot, slot, zs.at[c, i], zr.at[c, i], at_z(i))
             cp.start()
-            cps.append(cp)
+            cps[i] = cp
         return cps
 
-    def region(c, xx, hh, s, r, to):
-        cp = remote(g.at[c, xx, hh], g.at[c, xx, hh], s, r, to)
+    pushed = {}
+
+    def push(c, i, dx, dh, to, rdx, rdh):
+        slot = g.at[c, lax.rem(x + 4 - dx, 4), lax.rem(yh + dh, 2), lax.rem(z + 8 - i, 8)]
+        cp = remote(slot, slot, gs.at[c, rdh, rdx, i], gr.at[c, rdh, rdx, i], to)
         cp.start()
-        return cp
-
-    def spread(c):
-        first = region(c, x, yh, xs.at[c, 0], xr.at[c, 0], across)
-        return [first] + [
-            region(c, x, yh, xs.at[c, i], xr.at[c, i], at_x(i)) for i in (2, 1, 3)
-        ]
-
+        pushed[c, i, rdx, rdh] = cp
+
+    def arrived(c, i, dx, dh):
+        pushed[c, i, dx, dh].wait_recv()
+
+    right, left = at_x(1), at_x(3)
+
+    def step1(c, j, i):
+        if i:
+            zc[c][i].wait_recv()
+        push(c, i, 0, 0, across, 0, 1)
+        push(c, i, 0, 0, right, 1, 0)
+        push(c, i, 0, 0, left, 3, 0)
+
+    def y_last(c, j):
+        return j % 2 == 0 and not (c == 1 and j == 6)
+
+    def relay(c, j, i, dh):
+        arrived(c, i, 1, dh)
+        if j // 2 % 2 == 0:
+            push(c, i, 1, dh, right, 2, dh)
+        arrived(c, i, 3, dh)
+        if j // 2 % 2 == 1:
+            push(c, i, 3, dh, left, 2, dh)
+
+    def step2(c, j, i):
+        relay(c, j, i, 0)
+        if y_last(c, j):
+            push(c, i, 1, 0, across, 1, 1)
+            push(c, i, 3, 0, across, 3, 1)
+        arrived(c, i, 0, 1)
+        if not y_last(c, j):
+            push(c, i, 0, 1, right, 1, 1)
+            push(c, i, 0, 1, left, 3, 1)
+
+    def step3(c, j, i):
+        arrived(c, i, 2, 0)
+        if y_last(c, j):
+            push(c, i, 2, 0, across, 2, 1)
+            arrived(c, i, 1, 1)
+            arrived(c, i, 3, 1)
+        else:
+            relay(c, j, i, 1)
+
+    def step4(c, j, i):
+        arrived(c, i, 2, 1)
+
+    zc = {}
+
+    def begin(c):
+        for cp in red[c]:
+            cp.wait()
+        finish(c)
+        zc[c] = along_z(c)
+
+    events = [(4.9, 0, begin, (1,))]
+    for c in range(2):
+        for j, i in enumerate((0, 1, 7, 2, 6, 3, 5, 4)):
+            for n, step in enumerate((step1, step2, step3, step4)):
+                events.append((5 * c + j + 3 * n, n, step, (c, j, i)))
+    events.sort(key=lambda e: (e[0], -e[1]))
+
+    red = {}
     sums(0)
-    red0 = reduce_start(0)
+    red[0] = reduce_start(0)
     sums(1)
-    red1 = reduce_start(1)
-    for cp in red0:
-        cp.wait()
-    finish(0)
-    z0 = along_z(0)
-    for cp in red1:
-        cp.wait()
-    finish(1)
-    z1 = along_z(1)
-    for cp in z0:
-        cp.wait()
-    s0 = spread(0)
-    for cp in z1:
-        cp.wait()
-    s1 = spread(1)
-    fwd = []
-    s1[0].wait_recv()
-    for i in (2, 1, 3):
-        fwd.append(region(1, x, 1 - yh, fs.at[1, i], fr.at[1, i], at_x(i)))
-    for n, i in ((2, 1), (3, 3), (1, 2)):
-        s0[n].wait_recv()
-        xx = lax.rem(x + 4 - i, 4)
-        fwd.append(region(0, xx, yh, fs.at[0, i], fr.at[0, i], across))
-    s0[0].wait_recv()
-    for cp in s1[1:]:
-        cp.wait_recv()
-    for cp in s0 + s1:
+    red[1] = reduce_start(1)
+    begin(0)
+    for _, _, call, args in events:
+        call(*args)
+    for c in range(2):
+        for cp in zc[c].values():
+            cp.wait_send()
+    for cp in pushed.values():
         cp.wait_send()
-    for cp in fwd:
-        cp.wait()
 
 
 def widen_kernel(g, out):
+    z = pl.program_id(0)
     for c in range(2):
-        for hh in range(2):
-            at = (hh * 2 + c) * 128
-            out[:, at : at + 128] = g[c, 0, hh, 0].astype(F32)
+        for xx in range(4):
+            for hh in range(2):
+                at = (xx * 4 + hh * 2 + c) * 128
+                out[:, at : at + 128] = g[c, xx, hh, z].astype(F32)
 
 
 def per_device(points, centroids):
@@ -258,9 +322,10 @@
             jax.ShapeDtypeStruct((2, 4, 2, 8, D, 128), BF),
             jax.ShapeDtypeStruct((1, 128), F32),
         ],
-        in_specs=[vmem, pl.BlockSpec(memory_space=pl.ANY)],
+        in_specs=[pl.BlockSpec(memory_space=pltpu.HBM)] * 2,
         out_specs=[vmem, vmem],
         scratch_shapes=[
+            pltpu.VMEM((D, 128), BF),
             pltpu.VMEM((2, D, HALF), BF),
             pltpu.VMEM((D, 2048), BF),
             pltpu.VMEM((2048, 128), BF),
@@ -273,10 +338,10 @@
             pltpu.VMEM((16, 1, HALF), F32),
             pltpu.VMEM((2, 1, HALF), F32),
             pltpu.VMEM((2, 8, 104, 128), F32),
-            pltpu.VMEM((2, 8, 104, 128), F32),
-            dma((16,)), dma((16,)), dma((16,)), dma((3,)), dma((3,)), dma((16,)), dma((16,)),
-            dma((2, 8)), dma((2, 8)), dma((2, 8)), dma((2, 8)), dma((2, 4)), dma((2, 4)),
-            dma((2, 4)), dma((2, 4)),
+            pltpu.VMEM((2, 8, 112, 128), BF),
+            pltpu.VMEM((2, 8, 112, 128), BF),
+            dma((17,)), dma((16,)), dma((16,)), dma((7,)), dma((7,)), dma((16,)), dma((16,)),
+            dma((2, 8)), dma((2, 8)), dma((2, 8)), dma((2, 8)), dma((2, 2, 4, 8)), dma((2, 2, 4, 8)),
         ],
         compiler_params=pltpu.CompilerParams(
             collective_id=0, has_side_effects=True, vmem_limit_bytes=48 * 2**20
@@ -285,10 +350,11 @@
     )(points, centroids)
     whole = pl.pallas_call(
         widen_kernel,
-        grid=(8, 4),
+        grid=(8,),
         out_shape=jax.ShapeDtypeStruct((D, 16384), F32),
-        in_specs=[pl.BlockSpec((2, 1, 2, 1, D, 128), lambda z, x: (0, x, 0, z, 0, 0))],
-        out_specs=pl.BlockSpec((D, 512), lambda z, x: (0, z * 4 + x)),
+        in_specs=[vmem],
+        out_specs=pl.BlockSpec((D, 2048), lambda z: (0, z)),
+        compiler_params=pltpu.CompilerParams(vmem_limit_bytes=8 * 2**20),
         name="widen",
     )(g)
     return (whole, own_log.reshape(128))

time: 115 us -> 88.5 us (0.77)
  Pallas kernels: 110 us -> 86.2 us
  local copies, waits for them, and re-layouts: 2.89 us -> 1.24 us
    pallas_call x1, Pallas kernels: 18 us -> 4.09 us  [per_device(): pl.pallas_call(widen_kernel, grid=(8,), out_shape=jax.ShapeDtypeStruct((D...]
    pallas_call x1, Pallas kernels: 92.3 us -> 82.1 us  [per_device(): pl.pallas_call(em_kernel, out_shape=[jax.ShapeDtypeStruct((2, 4, 2, 8, D,...]
    unnamed x5 -> x3, local copies, waits for them, and re-layouts: 2.89 us -> 1.24 us
where the time goes in v3:
time: 88.5 us; the launch traced here: 88 us
  Pallas kernels  86.2 us (97%)
  local copies, waits for them, and re-layouts  1.24 us (1%)
    pallas_call x1, Pallas kernels, per_device(): pl.pallas_call(em_kernel, out_shape=[jax.ShapeDtypeStruct((2, 4, 2, 8, D,...  82.1 us
    pallas_call x1, Pallas kernels, per_device(): pl.pallas_call(widen_kernel, grid=(8,), out_shape=jax.ShapeDtypeStruct((D...  4.09 us

profile of v3, /device:TPU:2, one launch (start us, length us, event | category | flops | bytes accessed | tf_op | source)
XLA Modules:
  0.0 88.0 jit_solution(11193202890651756777)
XLA Ops:
  0.6 0.0 copy-start
  0.6 0.7 copy-done
  1.4 82.1 %em.1 = (bf16[2,4,2,8,96,128]{5,4,3,2,1,0:T(8,128)(2,1)S(1)}, f32[1,128]{1,0:T(1,128)S(1)}) custom-call(bf16[96,128]{1,0:T(8,128)(2,1)S(1)} %copy-done, bf16[96,16384]{1,0:T(8,128)(2,1)} %cents.1), custom_call_target="tpu_custom_call" | custom-call | tf_op jit(solution)/shard_map/em/pallas_call | solution.py:319
  83.5 4.1 %widen.1 = f32[96,16384]{1,0:T(8,128)} custom-call(bf16[2,4,2,8,96,128]{5,4,3,2,1,0:T(8,128)(2,1)S(1)} %get-tuple-element.4.g), custom_call_target="tpu_custom_call" | custom-call | tf_op jit(solution)/shard_map/widen/pallas_call | solution.py:351
  87.5 0.5 copy.5
Async XLA Ops:
  0.6 0.7 copy-start

commit v4 on v3

--- a/solution.py
+++ b/solution.py
@@ -16,6 +16,8 @@
 AXES = ("yl", "core", "z", "x", "yh")
 MESH = pl.DeviceIdType.MESH
 D = 96
+ARRIVAL = (0, 1, 7, 2, 6, 3, 5, 4)
+GROUP = 2
 HALF = 2048
 BF = jnp.bfloat16
 F32 = jnp.float32
@@ -65,18 +67,6 @@
     peers = [at_plane(i) for i in range(1, 16)] + [other] + [at_z(i) for i in range(1, 8)]
     for to in peers:
         pl.semaphore_signal(barrier, inc=1, device_id=to, device_id_type=MESH)
-    pl.semaphore_wait(barrier, len(peers))
-
-    mine = pl.ds(pl.multiple_of(chip * 128, 128), 128)
-    order = (1, 2, 3, 4, 5, 6, 7, 12, 13, 14, 15, 8, 9, 10, 11)
-    own.wait()
-    sends = {}
-    for i in order:
-        cp = remote(stage, pg.at[core, :, mine], ps.at[i], pr.at[i], at_plane(i))
-        cp.start()
-        sends[i] = cp
-    pg[core, :, mine] = stage[...]
-
     for cp in loads:
         cp.wait()
     ue[D:128, :] = jnp.where(
@@ -88,6 +78,17 @@
         ue[0:D, k : k + 512] = u
         full = jnp.concatenate([u.astype(F32), jnp.zeros((32, 512), F32)], axis=0)
         ut[k : k + 512, :] = full.T.astype(BF)
+    pl.semaphore_wait(barrier, len(peers))
+
+    mine = pl.ds(pl.multiple_of(chip * 128, 128), 128)
+    order = (1, 2, 3, 4, 5, 6, 7, 12, 13, 14, 15, 8, 9, 10, 11)
+    own.wait()
+    sends = {}
+    for i in order:
+        cp = remote(stage, pg.at[core, :, mine], ps.at[i], pr.at[i], at_plane(i))
+        cp.start()
+        sends[i] = cp
+    pg[core, :, mine] = stage[...]
 
     def column(k):
         return pl.ds(pl.multiple_of(lax.rem(x + 4 - k, 4) * 512, 512), 512)
@@ -96,9 +97,9 @@
         pts = pg[h, :, column(k)]
         top = jnp.full((8, 512), -1e30, F32)
         total = jnp.zeros((8, 512), F32)
-        for r in range(0, 2048, 256):
-            s = jnp.dot(ut[r : r + 256, 0:D], pts, preferred_element_type=F32)
-            s = s.reshape(32, 8, 512)
+        for r in range(0, 2048, 128):
+            s = jnp.dot(ut[r : r + 128, 0:D], pts, preferred_element_type=F32)
+            s = s.reshape(16, 8, 512)
             new = jnp.maximum(top, jnp.max(s, axis=0))
             e = jnp.exp2((s - new[None]) * SCALE)
             total = total * jnp.exp2((top - new) * SCALE) + jnp.sum(e, axis=0)
@@ -172,107 +173,109 @@
             f = jnp.where(row == 0, hi, jnp.where(row == 1, mid, jnp.where(row == 2, low, 0.0)))
             ptst[h * HALF + k : h * HALF + k + 512, D:128] = f.T.astype(BF)
 
+    first = lax.broadcasted_iota(jnp.int32, (16, 512), 0) == 0
+
+    def owner(c, i):
+        return pl.ds(pl.multiple_of(c * 1024 + lax.rem(z + i, 8) * 128, 128), 128)
+
     def sums(c):
-        for q in range(2):
-            at = c * 1024 + q * 512
-            uk = ue[:, at : at + 512]
-
-            def block(j, acc):
-                n = pl.ds(pl.multiple_of(j * 1024, 1024), 1024)
-                m = pl.ds(pl.multiple_of(lax.rem(j, 2) * 1024, 1024), 1024)
-                s = jnp.dot(ptst[n, :], uk, preferred_element_type=F32)
+        cps = []
+        for near in ((4, 3, 5, 2), (6, 1, 7, 0)):
+            uk = jnp.concatenate([ue[:, owner(c, i)] for i in near], axis=1)
+            acc = jnp.zeros((112, 512), F32)
+            for h in range(2):
+                s = jnp.dot(ptst[h * HALF : h * HALF + HALF, :], uk, preferred_element_type=F32)
                 e = jnp.exp2(s * SCALE).astype(BF)
-                return acc + jnp.dot(pe[j // 2, :, m], e, preferred_element_type=F32)
-
-            acc = lax.fori_loop(0, 4, block, jnp.zeros((112, 512), F32))
+                acc = acc + jnp.dot(pe[h], e, preferred_element_type=F32)
             tail = acc[D:112]
             hi = tail.astype(BF).astype(F32)
-            first = lax.broadcasted_iota(jnp.int32, (16, 512), 0) == 0
             parts = jnp.where(first, hi, tail - hi).astype(BF)
-            for k in range(4):
+            for k, i in enumerate(near):
                 at = slice(k * 128, k * 128 + 128)
-                w[c, q * 4 + k] = acc[0:104, at]
-                wb[c, q * 4 + k, 0:D] = acc[0:D, at].astype(BF)
-                wb[c, q * 4 + k, D:112] = parts[:, at]
-
-    def reduce_start(c):
-        cps = []
-        for i in (4, 3, 5, 2, 6, 1, 7):
-            zz = lax.rem(z + i, 8)
-            cp = remote(wb.at[c, zz], rxr.at[c, i], rs.at[c, i], rr.at[c, i], at_z(i))
-            cp.start()
-            cps.append(cp)
+                if i == 0:
+                    w[c] = acc[0:104, at]
+                    continue
+                wb[c, i, 0:D] = acc[0:D, at].astype(BF)
+                wb[c, i, D:112] = parts[:, at]
+                cp = remote(wb.at[c, i], rxr.at[c, i], rs.at[c, i], rr.at[c, i], at_z(i))
+                cp.start()
+                cps.append(cp)
         return cps
 
     def finish(c):
-        acc = w[c, z]
+        acc = w[c]
         for i in range(1, 8):
             acc = acc + rxr[c, i, 0:104].astype(F32)
-        sums, mass = acc[0:D], acc[D : D + 1] + (acc[D + 1 : D + 2] - w[c, z, D + 1 : D + 2])
-        u = ue[0:D, pl.ds(pl.multiple_of(c * 1024 + z * 128, 128), 128)].astype(F32)
-        g[c, x, yh, z] = ((sums + PRIOR_MASS * u) / (mass + PRIOR_MASS)).astype(BF)
+        sums, mass = acc[0:D], acc[D : D + 1] + (acc[D + 1 : D + 2] - w[c, D + 1 : D + 2])
+        u = ue[0:D, owner(c, 0)].astype(F32)
+        g[c, 0, 0, 0] = ((sums + PRIOR_MASS * u) / (mass + PRIOR_MASS)).astype(BF)
 
     def along_z(c):
         cps = {}
-        for i in (1, 7, 2, 6, 3, 5, 4):
-            slot = g.at[c, x, yh, z]
-            cp = remote(slot, slot, zs.at[c, i], zr.at[c, i], at_z(i))
+        for j in range(1, 8):
+            slot = g.at[c, 0, 0, j]
+            cp = remote(g.at[c, 0, 0, 0], slot, zs.at[c, j], zr.at[c, j], at_z(ARRIVAL[j]))
             cp.start()
-            cps[i] = cp
+            cps[j] = cp
         return cps
 
     pushed = {}
 
-    def push(c, i, dx, dh, to, rdx, rdh):
-        slot = g.at[c, lax.rem(x + 4 - dx, 4), lax.rem(yh + dh, 2), lax.rem(z + 8 - i, 8)]
-        cp = remote(slot, slot, gs.at[c, rdh, rdx, i], gr.at[c, rdh, rdx, i], to)
+    def push(c, n, dx, dh, to, rdx, rdh):
+        js = pl.ds(n * GROUP, GROUP)
+        cp = remote(
+            g.at[c, dh, dx, js], g.at[c, rdh, rdx, js], gs.at[c, rdh, rdx, n], gr.at[c, rdh, rdx, n], to
+        )
         cp.start()
-        pushed[c, i, rdx, rdh] = cp
-
-    def arrived(c, i, dx, dh):
-        pushed[c, i, dx, dh].wait_recv()
+        pushed[c, n, rdx, rdh] = cp
+
+    def arrived(c, n, dx, dh):
+        pushed[c, n, dx, dh].wait_recv()
 
     right, left = at_x(1), at_x(3)
 
-    def step1(c, j, i):
-        if i:
-            zc[c][i].wait_recv()
-        push(c, i, 0, 0, across, 0, 1)
-        push(c, i, 0, 0, right, 1, 0)
-        push(c, i, 0, 0, left, 3, 0)
-
-    def y_last(c, j):
-        return j % 2 == 0 and not (c == 1 and j == 6)
-
-    def relay(c, j, i, dh):
-        arrived(c, i, 1, dh)
-        if j // 2 % 2 == 0:
-            push(c, i, 1, dh, right, 2, dh)
-        arrived(c, i, 3, dh)
-        if j // 2 % 2 == 1:
-            push(c, i, 3, dh, left, 2, dh)
-
-    def step2(c, j, i):
-        relay(c, j, i, 0)
-        if y_last(c, j):
-            push(c, i, 1, 0, across, 1, 1)
-            push(c, i, 3, 0, across, 3, 1)
-        arrived(c, i, 0, 1)
-        if not y_last(c, j):
-            push(c, i, 0, 1, right, 1, 1)
-            push(c, i, 0, 1, left, 3, 1)
-
-    def step3(c, j, i):
-        arrived(c, i, 2, 0)
-        if y_last(c, j):
-            push(c, i, 2, 0, across, 2, 1)
-            arrived(c, i, 1, 1)
-            arrived(c, i, 3, 1)
+    def y_last(c, n):
+        return n % 2 == 0
+
+    def relay(c, n, dh):
+        if (c + n) % 2 == 0:
+            arrived(c, n, 1, dh)
+            push(c, n, 1, dh, right, 2, dh)
+            arrived(c, n, 3, dh)
         else:
-            relay(c, j, i, 1)
-
-    def step4(c, j, i):
-        arrived(c, i, 2, 1)
+            arrived(c, n, 3, dh)
+            push(c, n, 3, dh, left, 2, dh)
+            arrived(c, n, 1, dh)
+
+    def step1(c, n):
+        for j in range(n * GROUP, n * GROUP + GROUP):
+            if j:
+                zc[c][j].wait_recv()
+        push(c, n, 0, 0, across, 0, 1)
+        push(c, n, 0, 0, right, 1, 0)
+        push(c, n, 0, 0, left, 3, 0)
+
+    def step2(c, n):
+        relay(c, n, 0)
+        if y_last(c, n):
+            push(c, n, 1, 0, across, 1, 1)
+            push(c, n, 3, 0, across, 3, 1)
+        arrived(c, n, 0, 1)
+        if not y_last(c, n):
+            push(c, n, 0, 1, right, 1, 1)
+            push(c, n, 0, 1, left, 3, 1)
+
+    def step3(c, n):
+        arrived(c, n, 2, 0)
+        if y_last(c, n):
+            push(c, n, 2, 0, across, 2, 1)
+            arrived(c, n, 1, 1)
+            arrived(c, n, 3, 1)
+        else:
+            relay(c, n, 1)
+
+    def step4(c, n):
+        arrived(c, n, 2, 1)
 
     zc = {}
 
@@ -284,16 +287,14 @@
 
     events = [(4.9, 0, begin, (1,))]
     for c in range(2):
-        for j, i in enumerate((0, 1, 7, 2, 6, 3, 5, 4)):
-            for n, step in enumerate((step1, step2, step3, step4)):
-                events.append((5 * c + j + 3 * n, n, step, (c, j, i)))
+        for n in range(8 // GROUP):
+            for k, step in enumerate((step1, step2, step3, step4)):
+                events.append((5 * c + GROUP * n + 6 * k, k, step, (c, n)))
     events.sort(key=lambda e: (e[0], -e[1]))
 
     red = {}
-    sums(0)
-    red[0] = reduce_start(0)
-    sums(1)
-    red[1] = reduce_start(1)
+    red[0] = sums(0)
+    red[1] = sums(1)
     begin(0)
     for _, _, call, args in events:
         call(*args)
@@ -304,13 +305,25 @@
         cp.wait_send()
 
 
-def widen_kernel(g, out):
-    z = pl.program_id(0)
-    for c in range(2):
+def widen_kernel(g, log, out, log_out, buf, sem):
+    mz, mx, mh = lax.axis_index("z"), lax.axis_index("x"), lax.axis_index("yh")
+    cps = []
+    for z in range(8):
+        i = lax.rem(mz + 8 - z, 8)
+        j = jnp.where(i == 0, 0, jnp.where(i <= 4, 2 * i - 1, 16 - 2 * i))
         for xx in range(4):
-            for hh in range(2):
-                at = (xx * 4 + hh * 2 + c) * 128
-                out[:, at : at + 128] = g[c, xx, hh, z].astype(F32)
+            dx = lax.rem(mx + 4 - xx, 4)
+            for k in range(4):
+                dh = lax.rem(mh + k // 2, 2)
+                at = (z * 16 + xx * 4 + k) * 128
+                buf[:, at : at + 128] = g[k % 2, dh, dx, j].astype(F32)
+        at = slice(z * 2048, z * 2048 + 2048)
+        cp = pltpu.make_async_copy(buf.at[:, at], out.at[:, at], sem.at[z])
+        cp.start()
+        cps.append(cp)
+    log_out[...] = log[0]
+    for cp in cps:
+        cp.wait()
 
 
 def per_device(points, centroids):
@@ -319,7 +332,7 @@
     g, own_log = pl.pallas_call(
         em_kernel,
         out_shape=[
-            jax.ShapeDtypeStruct((2, 4, 2, 8, D, 128), BF),
+            jax.ShapeDtypeStruct((2, 2, 4, 8, D, 128), BF),
             jax.ShapeDtypeStruct((1, 128), F32),
         ],
         in_specs=[pl.BlockSpec(memory_space=pltpu.HBM)] * 2,
@@ -337,27 +350,29 @@
             pltpu.VMEM((1, HALF), F32),
             pltpu.VMEM((16, 1, HALF), F32),
             pltpu.VMEM((2, 1, HALF), F32),
-            pltpu.VMEM((2, 8, 104, 128), F32),
+            pltpu.VMEM((2, 104, 128), F32),
             pltpu.VMEM((2, 8, 112, 128), BF),
             pltpu.VMEM((2, 8, 112, 128), BF),
             dma((17,)), dma((16,)), dma((16,)), dma((7,)), dma((7,)), dma((16,)), dma((16,)),
-            dma((2, 8)), dma((2, 8)), dma((2, 8)), dma((2, 8)), dma((2, 2, 4, 8)), dma((2, 2, 4, 8)),
+            dma((2, 8)), dma((2, 8)), dma((2, 8)), dma((2, 8)), dma((2, 2, 4, 8 // GROUP)), dma((2, 2, 4, 8 // GROUP)),
         ],
         compiler_params=pltpu.CompilerParams(
             collective_id=0, has_side_effects=True, vmem_limit_bytes=48 * 2**20
         ),
         name="em",
     )(points, centroids)
-    whole = pl.pallas_call(
+    return pl.pallas_call(
         widen_kernel,
-        grid=(8,),
-        out_shape=jax.ShapeDtypeStruct((D, 16384), F32),
-        in_specs=[vmem],
-        out_specs=pl.BlockSpec((D, 2048), lambda z: (0, z)),
-        compiler_params=pltpu.CompilerParams(vmem_limit_bytes=8 * 2**20),
+        out_shape=[
+            jax.ShapeDtypeStruct((D, 16384), F32),
+            jax.ShapeDtypeStruct((128,), F32),
+        ],
+        in_specs=[vmem, vmem],
+        out_specs=[pl.BlockSpec(memory_space=pltpu.HBM), vmem],
+        scratch_shapes=[pltpu.VMEM((D, 16384), F32), dma((8,))],
+        compiler_params=pltpu.CompilerParams(vmem_limit_bytes=12 * 2**20),
         name="widen",
-    )(g)
-    return (whole, own_log.reshape(128))
+    )(g, own_log)
 
 
 def solution(mesh):

time: 88.5 us -> 84.1 us (0.950)
  Pallas kernels: 86.2 us -> 82.3 us
    pallas_call x2, Pallas kernels: 86.2 us -> 82.3 us  [the longest x1 79 us: per_device(): pl.pallas_call(em_kernel, out_shape=[jax.ShapeDtypeStruct((2, 2, 4, 8, D,...]
where the time goes in v4:
time: 84.1 us; the launch traced here: 83.9 us
  Pallas kernels  82.3 us (98%)
    pallas_call x1, Pallas kernels, per_device(): pl.pallas_call(em_kernel, out_shape=[jax.ShapeDtypeStruct((2, 2, 4, 8, D,...  79 us
    pallas_call x1, Pallas kernels, per_device(): pl.pallas_call(widen_kernel, out_shape=[jax.ShapeDtypeStruct((D, 16384),...  3.34 us

profile of v4, /device:TPU:2, one launch (start us, length us, event | category | flops | bytes accessed | tf_op | source)
XLA Modules:
  0.0 83.9 jit_solution(14275999937464030533)
XLA Ops:
  0.6 0.0 copy-start
  0.6 0.7 copy-done
  1.4 79.0 %em.1 = (bf16[2,2,4,8,96,128]{5,4,3,2,1,0:T(8,128)(2,1)S(1)}, f32[1,128]{1,0:T(1,128)S(1)}) custom-call(bf16[96,128]{1,0:T(8,128)(2,1)S(1)} %copy-done, bf16[96,16384]{1,0:T(8,128)(2,1)} %cents.1), custom_call_target="tpu_custom_call" | custom-call | tf_op jit(solution)/shard_map/em/pallas_call | solution.py:332
  80.4 3.3 %widen.1 = (f32[96,16384]{1,0:T(8,128)}, f32[128]{0:T(128)}) custom-call(bf16[2,2,4,8,96,128]{5,4,3,2,1,0:T(8,128)(2,1)S(1)} %get-tuple-element.4.g, f32[1,128]{1,0:T(1,128)S(1)} %get-tuple-element.5.log), custom_call_target="tpu_custom_call" | custom-call | tf_op jit(solution)/shard_map/widen/pallas_call | solution.py:364
Async XLA Ops:
  0.6 0.7 copy-start

commit v5 on v4

--- a/solution.py
+++ b/solution.py
@@ -18,15 +18,16 @@
 D = 96
 ARRIVAL = (0, 1, 7, 2, 6, 3, 5, 4)
 GROUP = 2
+RA = 32
 HALF = 2048
 BF = jnp.bfloat16
 F32 = jnp.float32
 
 
 def em_kernel(
-    points, cents, g, own_log,
+    points, cents, ga, g, own_log,
     stage, pg, cu, ut, ue, ptst, pe, lp, rxa, cb, rxb, lo, w, wb, rxr,
-    cu_sem, ps, pr, ds, dr, bs, br, rs, rr, zs, zr, gs, gr,
+    cu_sem, ps, pr, ds, dr, bs, br, rs, rr, zs, zr, gs, gr, as_, ar, rs_, rr_,
 ):
     yl, core, z, x, yh = [lax.axis_index(a) for a in AXES]
     y = yh * 2 + yl
@@ -208,7 +209,9 @@
             acc = acc + rxr[c, i, 0:104].astype(F32)
         sums, mass = acc[0:D], acc[D : D + 1] + (acc[D + 1 : D + 2] - w[c, D + 1 : D + 2])
         u = ue[0:D, owner(c, 0)].astype(F32)
-        g[c, 0, 0, 0] = ((sums + PRIOR_MASS * u) / (mass + PRIOR_MASS)).astype(BF)
+        fresh = ((sums + PRIOR_MASS * u) / (mass + PRIOR_MASS)).astype(BF)
+        ga[c, 0, 0] = fresh[0:RA]
+        g[c, 0, 0, 0] = fresh[RA:D]
 
     def along_z(c):
         cps = {}
@@ -218,6 +221,46 @@
             cp.start()
             cps[j] = cp
         return cps
+
+    plane, ring = {}, {}
+
+    def at_xy(dx, dh):
+        return (yl, core, z, lax.rem(x + dx, 4), lax.rem(yh + dh, 2))
+
+    def over_plane(c):
+        plane[c] = []
+        for n in (6, 2, 7, 5, 4, 3, 1):
+            cp = remote(
+                ga.at[c, 0, 0], ga.at[c, 0, n], as_.at[c, n], ar.at[c, n], at_xy(n % 4, n // 4)
+            )
+            cp.start()
+            plane[c].append(cp)
+
+    def hop(c, i, to):
+        src, dst = i, (i + to) % 8
+        j = ARRIVAL.index(dst)
+        cp = remote(
+            ga.at[c, ARRIVAL.index(src)], ga.at[c, j], rs_.at[c, j], rr_.at[c, j], at_z(to % 8)
+        )
+        cp.start()
+        ring[c, dst] = cp
+
+    def ring_step(c, n):
+        if n == 0:
+            for cp in plane[c]:
+                cp.wait_recv()
+            hop(c, 0, 1)
+            hop(c, 0, -1)
+        elif n < 4:
+            up, down = n, 8 - n
+            ring[c, up].wait_recv()
+            if n < 3 or c == 0:
+                hop(c, up, 1)
+            ring[c, down].wait_recv()
+            if n < 3 or c == 1:
+                hop(c, down, -1)
+        else:
+            ring[c, 4].wait_recv()
 
     pushed = {}
 
@@ -283,6 +326,7 @@
         for cp in red[c]:
             cp.wait()
         finish(c)
+        over_plane(c)
         zc[c] = along_z(c)
 
     events = [(4.9, 0, begin, (1,))]
@@ -290,6 +334,8 @@
         for n in range(8 // GROUP):
             for k, step in enumerate((step1, step2, step3, step4)):
                 events.append((5 * c + GROUP * n + 6 * k, k, step, (c, n)))
+        for n in range(5):
+            events.append((5 * c + 4.5 + 4 * n, 9, ring_step, (c, n)))
     events.sort(key=lambda e: (e[0], -e[1]))
 
     red = {}
@@ -301,11 +347,13 @@
     for c in range(2):
         for cp in zc[c].values():
             cp.wait_send()
-    for cp in pushed.values():
+        for cp in plane[c]:
+            cp.wait_send()
+    for cp in list(pushed.values()) + list(ring.values()):
         cp.wait_send()
 
 
-def widen_kernel(g, log, out, log_out, buf, sem):
+def widen_kernel(ga, g, log, out, log_out, buf, sem):
     mz, mx, mh = lax.axis_index("z"), lax.axis_index("x"), lax.axis_index("yh")
     cps = []
     for z in range(8):
@@ -316,7 +364,8 @@
             for k in range(4):
                 dh = lax.rem(mh + k // 2, 2)
                 at = (z * 16 + xx * 4 + k) * 128
-                buf[:, at : at + 128] = g[k % 2, dh, dx, j].astype(F32)
+                buf[0:RA, at : at + 128] = ga[k % 2, j, dh * 4 + dx].astype(F32)
+                buf[RA:D, at : at + 128] = g[k % 2, dh, dx, j].astype(F32)
         at = slice(z * 2048, z * 2048 + 2048)
         cp = pltpu.make_async_copy(buf.at[:, at], out.at[:, at], sem.at[z])
         cp.start()
@@ -329,14 +378,15 @@
 def per_device(points, centroids):
     vmem = pl.BlockSpec(memory_space=pltpu.VMEM)
     dma = pltpu.SemaphoreType.DMA
-    g, own_log = pl.pallas_call(
+    ga, g, own_log = pl.pallas_call(
         em_kernel,
         out_shape=[
-            jax.ShapeDtypeStruct((2, 2, 4, 8, D, 128), BF),
+            jax.ShapeDtypeStruct((2, 8, 8, RA, 128), BF),
+            jax.ShapeDtypeStruct((2, 2, 4, 8, D - RA, 128), BF),
             jax.ShapeDtypeStruct((1, 128), F32),
         ],
         in_specs=[pl.BlockSpec(memory_space=pltpu.HBM)] * 2,
-        out_specs=[vmem, vmem],
+        out_specs=[vmem] * 3,
         scratch_shapes=[
             pltpu.VMEM((D, 128), BF),
             pltpu.VMEM((2, D, HALF), BF),
@@ -355,6 +405,7 @@
             pltpu.VMEM((2, 8, 112, 128), BF),
             dma((17,)), dma((16,)), dma((16,)), dma((7,)), dma((7,)), dma((16,)), dma((16,)),
             dma((2, 8)), dma((2, 8)), dma((2, 8)), dma((2, 8)), dma((2, 2, 4, 8 // GROUP)), dma((2, 2, 4, 8 // GROUP)),
+            dma((2, 8)), dma((2, 8)), dma((2, 8)), dma((2, 8)),
         ],
         compiler_params=pltpu.CompilerParams(
             collective_id=0, has_side_effects=True, vmem_limit_bytes=48 * 2**20
@@ -367,12 +418,12 @@
             jax.ShapeDtypeStruct((D, 16384), F32),
             jax.ShapeDtypeStruct((128,), F32),
         ],
-        in_specs=[vmem, vmem],
+        in_specs=[vmem] * 3,
         out_specs=[pl.BlockSpec(memory_space=pltpu.HBM), vmem],
         scratch_shapes=[pltpu.VMEM((D, 16384), F32), dma((8,))],
         compiler_params=pltpu.CompilerParams(vmem_limit_bytes=12 * 2**20),
         name="widen",
-    )(g, own_log)
+    )(ga, g, own_log)
 
 
 def solution(mesh):

time: 84.1 us -> 82.5 us (0.981)
  the two profiles are of different devices: /device:TPU:2 before, /device:TPU:32 now
where the time goes in v5:
time: 82.5 us; the launch traced here: 82.3 us
  Pallas kernels  80.7 us (98%)
    pallas_call x1, Pallas kernels, per_device(): pl.pallas_call(em_kernel, out_shape=[jax.ShapeDtypeStruct((2, 8, 8, RA, 1...  77.4 us
    pallas_call x1, Pallas kernels, per_device(): pl.pallas_call(widen_kernel, out_shape=[jax.ShapeDtypeStruct((D, 16384),...  3.34 us

profile of v5, /device:TPU:32, one launch (start us, length us, event | category | flops | bytes accessed | tf_op | source)
XLA Modules:
  0.0 82.3 jit_solution(10293734559352245037)
XLA Ops:
  0.6 0.0 copy-start
  0.6 0.7 copy-done
  1.4 77.4 %em.1 = (bf16[2,8,8,32,128]{4,3,2,1,0:T(8,128)(2,1)S(1)}, bf16[2,2,4,8,64,128]{5,4,3,2,1,0:T(8,128)(2,1)S(1)}, f32[1,128]{1,0:T(1,128)S(1)}) custom-call(bf16[96,128]{1,0:T(8,128)(2,1)S(1)} %copy-done, bf16[96,16384]{1,0:T(8,128)(2,1)} %cents.1), custom_call_target="tpu_custom_call" | custom-call | tf_op jit(solution)/shard_map/em/pallas_call | solution.py:381
  78.8 3.3 %widen.1 = (f32[96,16384]{1,0:T(8,128)}, f32[128]{0:T(128)}) custom-call(bf16[2,8,8,32,128]{4,3,2,1,0:T(8,128)(2,1)S(1)} %get-tuple-element.5.ga, bf16[2,2,4,8,64,128]{5,4,3,2,1,0:T(8,128)(2,1)S(1)} %get-tuple-element.6.g, f32[1,128]{1,0:T(1,128)S(1)} %get-tuple-element.7.log), custom_call_target="tpu_custom_call" | custom-call | tf_op jit(solution)/shard_map/widen/pallas_call | solution.py:415
Async XLA Ops:
  0.6 0.7 copy-start

commit v6 on v5

--- a/solution.py
+++ b/solution.py
@@ -26,7 +26,7 @@
 
 def em_kernel(
     points, cents, ga, g, own_log,
-    stage, pg, cu, ut, ue, ptst, pe, lp, rxa, cb, rxb, lo, w, wb, rxr,
+    stage, pg, cu, ut, ue, ptst, pe, eb, lp, rxa, cb, rxb, lo, w, wb, rxr,
     cu_sem, ps, pr, ds, dr, bs, br, rs, rr, zs, zr, gs, gr, as_, ar, rs_, rr_,
 ):
     yl, core, z, x, yh = [lax.axis_index(a) for a in AXES]
@@ -130,10 +130,6 @@
 
     give = remote(lp.at[1 - core], rxa, ds.at[1], dr.at[1], other)
     give.start()
-    ones = jnp.where(lax.broadcasted_iota(jnp.int32, (16, HALF), 0) < 2, 1.0, 0.0).astype(BF)
-    for h in range(2):
-        pe[h, 0:D, :] = pg[h]
-        pe[h, D:112, :] = ones
     give.wait()
     a, b = lp[core], rxa[...]
     top = jnp.maximum(a, b)
@@ -150,6 +146,27 @@
                 [pg[h, :, k : k + 512].astype(F32), jnp.zeros((32, 512), F32)], axis=0
             )
             ptst[h * HALF + k : h * HALF + k + 512, :] = f.T.astype(BF)
+    row = lax.broadcasted_iota(jnp.int32, (32, 512), 0)
+    for h in range(2):
+        for k in range(0, HALF, 512):
+            v = lp[h, :, k : k + 512] * (-1.0 / SCALE)
+            hi = v.astype(BF).astype(F32)
+            mid = (v - hi).astype(BF).astype(F32)
+            low = v - hi - mid
+            f = jnp.where(row == 0, hi, jnp.where(row == 1, mid, jnp.where(row == 2, low, 0.0)))
+            ptst[h * HALF + k : h * HALF + k + 512, D:128] = f.T.astype(BF)
+
+    def owner(c, i):
+        return pl.ds(pl.multiple_of(c * 1024 + lax.rem(z + i, 8) * 128, 128), 128)
+
+    near = ((4, 3, 5, 2), (6, 1, 7, 0))
+    for c in range(2):
+        for q in range(2):
+            uk = jnp.concatenate([ue[:, owner(c, i)] for i in near[q]], axis=1)
+            for h in range(2):
+                at = slice(h * HALF, h * HALF + HALF)
+                s = jnp.dot(ptst[at, :], uk, preferred_element_type=F32)
+                eb[c, q, at, :] = jnp.exp2(s * SCALE).astype(BF)
     for cp in sends:
         cp.wait()
     top = rxb[0]
@@ -164,39 +181,36 @@
     own_log[...] = lo[core, :, mine] * LN2
     back.wait()
 
-    row = lax.broadcasted_iota(jnp.int32, (32, 512), 0)
+    mrow = lax.broadcasted_iota(jnp.int32, (16, 512), 0)
     for h in range(2):
         for k in range(0, HALF, 512):
-            v = lo[h, :, k : k + 512] * (-1.0 / SCALE)
-            hi = v.astype(BF).astype(F32)
-            mid = (v - hi).astype(BF).astype(F32)
-            low = v - hi - mid
-            f = jnp.where(row == 0, hi, jnp.where(row == 1, mid, jnp.where(row == 2, low, 0.0)))
-            ptst[h * HALF + k : h * HALF + k + 512, D:128] = f.T.astype(BF)
-
-    first = lax.broadcasted_iota(jnp.int32, (16, 512), 0) == 0
-
-    def owner(c, i):
-        return pl.ds(pl.multiple_of(c * 1024 + lax.rem(z + i, 8) * 128, 128), 128)
+            at = slice(k, k + 512)
+            f = jnp.exp2(lp[h, :, at] - lo[h, :, at])
+            v = pg[h, :, at].astype(F32) * f
+            hi = v.astype(BF)
+            pe[h, 0:D, at] = hi
+            pe[h, D : 2 * D, at] = (v - hi.astype(F32)).astype(BF)
+            fh = f.astype(BF).astype(F32)
+            pe[h, 2 * D : 208, at] = jnp.where(
+                mrow == 0, fh, jnp.where(mrow == 1, f - fh, 0.0)
+            ).astype(BF)
 
     def sums(c):
         cps = []
-        for near in ((4, 3, 5, 2), (6, 1, 7, 0)):
-            uk = jnp.concatenate([ue[:, owner(c, i)] for i in near], axis=1)
-            acc = jnp.zeros((112, 512), F32)
-            for h in range(2):
-                s = jnp.dot(ptst[h * HALF : h * HALF + HALF, :], uk, preferred_element_type=F32)
-                e = jnp.exp2(s * SCALE).astype(BF)
-                acc = acc + jnp.dot(pe[h], e, preferred_element_type=F32)
-            tail = acc[D:112]
-            hi = tail.astype(BF).astype(F32)
-            parts = jnp.where(first, hi, tail - hi).astype(BF)
-            for k, i in enumerate(near):
+        for q in range(2):
+            acc = jnp.dot(pe[0], eb[c, q, 0:HALF, :], preferred_element_type=F32)
+            acc = acc + jnp.dot(pe[1], eb[c, q, HALF : 2 * HALF, :], preferred_element_type=F32)
+            total = acc[0:D] + acc[D : 2 * D]
+            mass = acc[2 * D : 2 * D + 1] + acc[2 * D + 1 : 2 * D + 2]
+            hi = mass.astype(BF).astype(F32)
+            parts = jnp.where(mrow == 0, hi, jnp.where(mrow == 1, mass - hi, 0.0)).astype(BF)
+            for k, i in enumerate(near[q]):
                 at = slice(k * 128, k * 128 + 128)
                 if i == 0:
-                    w[c] = acc[0:104, at]
+                    w[c, 0:D] = total[:, at]
+                    w[c, D:104] = jnp.broadcast_to(mass[:, at], (8, 128))
                     continue
-                wb[c, i, 0:D] = acc[0:D, at].astype(BF)
+                wb[c, i, 0:D] = total[:, at].astype(BF)
                 wb[c, i, D:112] = parts[:, at]
                 cp = remote(wb.at[c, i], rxr.at[c, i], rs.at[c, i], rr.at[c, i], at_z(i))
                 cp.start()
@@ -394,7 +408,8 @@
             pltpu.VMEM((2048, 128), BF),
             pltpu.VMEM((128, 2048), BF),
             pltpu.VMEM((2 * HALF, 128), BF),
-            pltpu.VMEM((2, 112, HALF), BF),
+            pltpu.VMEM((2, 208, HALF), BF),
+            pltpu.VMEM((2, 2, 2 * HALF, 512), BF),
             pltpu.VMEM((2, 1, HALF), F32),
             pltpu.VMEM((1, HALF), F32),
             pltpu.VMEM((1, HALF), F32),

time: 82.5 us -> 79.2 us (0.960)
  the two profiles are of different devices: /device:TPU:32 before, /device:TPU:2 now
where the time goes in v6:
time: 79.2 us; the launch traced here: 78.4 us
  Pallas kernels  76.9 us (97%)
  between operations  0.81 us (1%)
    pallas_call x1, Pallas kernels, per_device(): pl.pallas_call(em_kernel, out_shape=[jax.ShapeDtypeStruct((2, 8, 8, RA, 1...  73.5 us
    pallas_call x1, Pallas kernels, per_device(): pl.pallas_call(widen_kernel, out_shape=[jax.ShapeDtypeStruct((D, 16384),...  3.33 us

profile of v6, /device:TPU:2, one launch (start us, length us, event | category | flops | bytes accessed | tf_op | source)
XLA Modules:
  0.0 78.4 jit_solution(5621647086635393919)
XLA Ops:
  0.6 0.0 copy-start
  0.6 0.7 copy-done
  1.4 73.5 %em.1 = (bf16[2,8,8,32,128]{4,3,2,1,0:T(8,128)(2,1)S(1)}, bf16[2,2,4,8,64,128]{5,4,3,2,1,0:T(8,128)(2,1)S(1)}, f32[1,128]{1,0:T(1,128)S(1)}) custom-call(bf16[96,128]{1,0:T(8,128)(2,1)S(1)} %copy-done, bf16[96,16384]{1,0:T(8,128)(2,1)} %cents.1), custom_call_target="tpu_custom_call" | custom-call | tf_op jit(solution)/shard_map/em/pallas_call | solution.py:395
  74.9 3.3 %widen.1 = (f32[96,16384]{1,0:T(8,128)}, f32[128]{0:T(128)}) custom-call(bf16[2,8,8,32,128]{4,3,2,1,0:T(8,128)(2,1)S(1)} %get-tuple-element.5.ga, bf16[2,2,4,8,64,128]{5,4,3,2,1,0:T(8,128)(2,1)S(1)} %get-tuple-element.6.g, f32[1,128]{1,0:T(1,128)S(1)} %get-tuple-element.7.log), custom_call_target="tpu_custom_call" | custom-call | tf_op jit(solution)/shard_map/widen/pallas_call | solution.py:430
Async XLA Ops:
  0.6 0.7 copy-start

commit v7 on v6

--- a/solution.py
+++ b/solution.py
@@ -160,13 +160,16 @@
         return pl.ds(pl.multiple_of(c * 1024 + lax.rem(z + i, 8) * 128, 128), 128)
 
     near = ((4, 3, 5, 2), (6, 1, 7, 0))
-    for c in range(2):
-        for q in range(2):
-            uk = jnp.concatenate([ue[:, owner(c, i)] for i in near[q]], axis=1)
-            for h in range(2):
-                at = slice(h * HALF, h * HALF + HALF)
-                s = jnp.dot(ptst[at, :], uk, preferred_element_type=F32)
-                eb[c, q, at, :] = jnp.exp2(s * SCALE).astype(BF)
+
+    def weigh(c, q):
+        uk = jnp.concatenate([ue[:, owner(c, i)] for i in near[q]], axis=1)
+        for h in range(2):
+            at = slice(h * HALF, h * HALF + HALF)
+            s = jnp.dot(ptst[at, :], uk, preferred_element_type=F32)
+            eb[c, q, at, :] = jnp.exp2(s * SCALE).astype(BF)
+
+    for c, q in ((0, 0), (0, 1), (1, 0)):
+        weigh(c, q)
     for cp in sends:
         cp.wait()
     top = rxb[0]
@@ -198,6 +201,8 @@
     def sums(c):
         cps = []
         for q in range(2):
+            if c == 1 and q == 1:
+                weigh(c, q)
             acc = jnp.dot(pe[0], eb[c, q, 0:HALF, :], preferred_element_type=F32)
             acc = acc + jnp.dot(pe[1], eb[c, q, HALF : 2 * HALF, :], preferred_element_type=F32)
             total = acc[0:D] + acc[D : 2 * D]

time: 79.2 us -> 79.8 us (level)
  no operation moved by 1% of the time
where the time goes in v7:
time: 79.8 us; the launch traced here: 78.6 us
  Pallas kernels  77 us (96%)
  between operations  0.81 us (1%)
    pallas_call x1, Pallas kernels, per_device(): pl.pallas_call(em_kernel, out_shape=[jax.ShapeDtypeStruct((2, 8, 8, RA, 1...  73.7 us
    pallas_call x1, Pallas kernels, per_device(): pl.pallas_call(widen_kernel, out_shape=[jax.ShapeDtypeStruct((D, 16384),...  3.33 us

profile of v7, /device:TPU:2, one launch (start us, length us, event | category | flops | bytes accessed | tf_op | source)
XLA Modules:
  0.0 78.6 jit_solution(12832813801979512912)
XLA Ops:
  0.6 0.0 copy-start
  0.6 0.7 copy-done
  1.4 73.7 %em.1 = (bf16[2,8,8,32,128]{4,3,2,1,0:T(8,128)(2,1)S(1)}, bf16[2,2,4,8,64,128]{5,4,3,2,1,0:T(8,128)(2,1)S(1)}, f32[1,128]{1,0:T(1,128)S(1)}) custom-call(bf16[96,128]{1,0:T(8,128)(2,1)S(1)} %copy-done, bf16[96,16384]{1,0:T(8,128)(2,1)} %cents.1), custom_call_target="tpu_custom_call" | custom-call | tf_op jit(solution)/shard_map/em/pallas_call | solution.py:400
  75.1 3.3 %widen.1 = (f32[96,16384]{1,0:T(8,128)}, f32[128]{0:T(128)}) custom-call(bf16[2,8,8,32,128]{4,3,2,1,0:T(8,128)(2,1)S(1)} %get-tuple-element.5.ga, bf16[2,2,4,8,64,128]{5,4,3,2,1,0:T(8,128)(2,1)S(1)} %get-tuple-element.6.g, f32[1,128]{1,0:T(1,128)S(1)} %get-tuple-element.7.log), custom_call_target="tpu_custom_call" | custom-call | tf_op jit(solution)/shard_map/widen/pallas_call | solution.py:435
Async XLA Ops:
  0.6 0.7 copy-start
